TPU v7x, 512 devices: a whole 4x4x16 slice. The times are simulated.
512 devices in a mesh: mp: 16 (over z_lo, y), dp: 32 (over z_hi, x, core).
Axes of the slice: x: 4, y: 4, z: 16 (z_hi: 4, z_lo: 4; z = z_hi * 4 + z_lo), core: 2. Of those that a mesh axis runs over, the one named last changes fastest.
Arguments:
- train_acts: bfloat16 [16, 128, 64, 3584], P('mp', 'dp'), may hold values from -6 to 6
- train_grads: bfloat16 [16, 128, 64, 2048], P('mp', 'dp'), may hold values from -6 to 6
- query_acts: bfloat16 [16, 64, 64, 3584], P('mp', 'dp'), may hold values from -6 to 6
- query_grads: bfloat16 [16, 64, 64, 2048], P('mp', 'dp'), may hold values from -6 to 6
- train_lengths: int32 [128], P('dp'), may hold values from 8 to 64, as said below
- query_lengths: int32 [64], P('dp'), may hold values from 8 to 64, as said below
- proj_salts: int32 [16, 2], P('mp'), may hold values from 0 to 99999
Outputs:
- scores: float32 [64, 128], P('dp', 'mp')
Inputs may be any that keep to these rules, and one draw needn't show every extreme that they name: `train_lengths`: some training example uses all 64 slots and some uses 64 // 8. `query_lengths`: some query example uses all 64 slots and some uses 64 // 8.
All inputs are finite; a program needn't handle non-finite values.
Results may differ from a plain program's by a relative error of at most 0.0003.
Values sent between devices are 32-bit elements; how exact they have to be, the bound alone decides.
A program may use at most 64 MiB of HBM per device.

v0:
```python
import jax
import jax.numpy as jnp
from jax import lax
from jax.sharding import PartitionSpec as P

R1 = 64
R2 = 64


RIDGE_SCALE = 0.1


def shift_down(value, amount):
    return lax.shift_right_logical(value, jnp.full_like(value, amount))


def sign_table(hash_salt, rows, cols):
    row_index = lax.broadcasted_iota(jnp.int32, (rows, cols), 0)
    col_index = lax.broadcasted_iota(jnp.int32, (rows, cols), 1)
    hashed = row_index * 73856093 + col_index * 19349663 + hash_salt * 83492791
    hashed = hashed ^ shift_down(hashed, 15)
    hashed = hashed * 1274126177
    hashed = hashed ^ shift_down(hashed, 13)
    hashed = hashed * 668265263
    hashed = hashed ^ shift_down(hashed, 16)
    bit_value = shift_down(hashed, 7) & 1
    signs = (bit_value * 2 - 1).astype(jnp.float32)
    return (signs * (1.0 / rows**0.5)).astype(jnp.bfloat16)


def project(activations, gradients, lengths, proj_in, proj_out):
    count, length, width = activations.shape
    left = jnp.dot(
        activations.reshape(count * length, width), proj_in, preferred_element_type=jnp.float32
    )
    right = jnp.dot(
        gradients.reshape(count * length, gradients.shape[2]),
        proj_out,
        preferred_element_type=jnp.float32,
    )
    left = left.reshape(count, length, proj_in.shape[1])
    right = right.reshape(count, length, proj_out.shape[1])
    positions = lax.broadcasted_iota(jnp.int32, (count, length), 1)
    token_mask = (positions < lengths[:, None]).astype(jnp.float32)
    left = left * token_mask[:, :, None]
    outer = jnp.einsum("elr,els->ers", left, right, precision=lax.Precision.HIGHEST)
    return outer.reshape(count, proj_in.shape[1] * proj_out.shape[1])


def inner_rows(first, second):
    return jnp.dot(
        first, second.T, precision=lax.Precision.HIGHEST, preferred_element_type=jnp.float32
    )


def shards(
    train_acts, train_grads, query_acts, query_grads, train_lengths, query_lengths, proj_salts
):
    local_ckpts = train_acts.shape[0]
    query_count = query_acts.shape[1]
    train_total = train_acts.shape[1] * lax.axis_size("dp")
    ckpt_total = local_ckpts * lax.axis_size("mp")
    total = jnp.zeros((query_count, train_total), jnp.float32)
    proj_in = sign_table(proj_salts[0, 0], train_acts.shape[3], R1)
    proj_out = sign_table(proj_salts[0, 1], train_grads.shape[3], R2)
    train_rows = project(train_acts[0], train_grads[0], train_lengths, proj_in, proj_out)
    query_rows = project(query_acts[0], query_grads[0], query_lengths, proj_in, proj_out)
    everyone = lax.all_gather(train_rows, "dp", axis=0, tiled=True)
    kernel = inner_rows(everyone, everyone)
    cross_terms = inner_rows(query_rows, everyone)
    ridge_term = RIDGE_SCALE * jnp.trace(kernel) / train_total
    system = kernel + ridge_term * jnp.eye(train_total, dtype=jnp.float32)
    factor = jnp.linalg.cholesky(system)
    solved = jax.scipy.linalg.cho_solve((factor, True), cross_terms.T).T
    total = total + solved
    summed = lax.psum(total, "mp")
    share_width = train_total // lax.axis_size("mp")
    share = lax.dynamic_slice_in_dim(summed, lax.axis_index("mp") * share_width, share_width, 1)
    return share * (train_total / ckpt_total)


def solution(mesh):
    placed = (
        P("mp", "dp", None, None),
        P("mp", "dp", None, None),
        P("mp", "dp", None, None),
        P("mp", "dp", None, None),
        P("dp"),
        P("dp"),
        P("mp", None),
    )
    return jax.shard_map(
        shards, mesh=mesh, in_specs=placed, out_specs=P("dp", "mp"), check_vma=False
    )
```

profile of v0, /device:TPU:2, one launch (start us, length us, event | category | flops | bytes accessed | tf_op | source)
XLA Modules:
  0.0 178.2 jit_solution(76525755539039017)
XLA Ops:
  6.6 1.5 fusion.74
  8.7 0.0 copy-start.2
  8.7 0.7 convolution_bitcast_fusion.1
  9.4 0.0 copy-start.1
  9.4 0.1 reshape.75
  10.2 0.6 convolution_bitcast_fusion
  10.8 0.1 copy.23
  10.9 0.1 fusion.33
  11.0 0.3 fusion.22
  11.2 0.7 reshape.81
  12.0 0.0 all-gather.3.cloned.1.call-update
  12.0 1.9 %convolution_bitcast_fusion.2 = f32[128,64]{0,1:T(8,128)S(1)} fusion(bf16[128,3584]{1,0:T(8,128)(2,1)} %bitcast.49, s32[]{:T(128)} %bitcast, s32[64]{0:T(128)S(1)} %iota_multiply_fusion.2, s32[3584]{0:T(1024)S(1)} %iota_multiply_fusion), kind=kOutput, calls=%fused_computation.5 | convolution fusion | flops 62619648 | bytes 964868 | tf_op jit(solution)/shard_map/dot_general | solution.py:33
  13.9 0.0 copy-start.4
  13.9 0.1 reshape.78
  14.0 0.5 convolution_bitcast_fusion.3
  14.5 0.1 copy.24
  14.6 0.1 compare_convert_fusion
  14.7 0.2 fusion.30
  14.9 0.1 reshape.80
  15.0 80.2 %all-gather.3.cloned.1.call-done = f32[32,4,4096]{2,1,0:T(4,128)} async-done(((f32[1,4,4096]{2,1,0:T(4,128)}), f32[32,4,4096]{2,1,0:T(4,128)}) %all-gather.3.cloned.1.call-update) | async-done | bytes 2097168 | tf_op jit(solution)/shard_map/all_gather | solution.py:68
  95.1 2.9 %reshape.82 = f32[128,4096]{1,0:T(8,128)} reshape(f32[32,4,4096]{2,1,0:T(4,128)} %all-gather.3.cloned.1.call-done) | data formatting | bytes 4194304
  98.1 4.7 %select_reduce_fusion.1 = (f32[]{:T(128)}, f32[128,128]{1,0:T(8,128)S(1)}) fusion(f32[128,4096]{1,0:T(8,128)} %reshape.82), kind=kOutput, calls=%fused_computation.43 | convolution fusion | flops 805355520 | bytes 2162692 | tf_op jit(solution)/shard_map/dot_general | solution.py:51
  102.7 0.1 copy.20
  103.5 11.7 %cholesky.17 = f32[128,128]{1,0:T(8,128)S(1)} custom-call(f32[128,128]{1,0:T(8,128)S(1)} %fusion.29), custom_call_target="Cholesky" | custom-call | tf_op jit(solution)/shard_map/jit(cholesky)/cholesky | solution.py:73
  115.3 0.6 compare_reduce_fusion
  115.9 0.7 fusion.23
  116.6 9.8 %custom-call.10 = f32[1,128,128]{1,2,0:T(8,128)S(1)} custom-call(f32[1,128,128]{2,1,0:T(8,128)S(1)} %fusion.23), custom_call_target="InvertDiagBlocksLowerTriangular" | custom-call | tf_op jit(solution)/shard_map/jit(_cho_solve)/triangular_solve | solution.py:74
  126.4 3.3 %fusion.75 = f32[128,2]{0,1:T(2,128)S(1)} fusion(f32[128,4096]{1,0:T(8,128)} %reshape.82, f32[2,4096]{1,0:T(2,128)S(1)} %reshape.80), kind=kOutput, calls=%fused_computation.97 | convolution fusion | flops 12582912 | bytes 2130944 | tf_op jit(solution)/shard_map/dot_general | solution.py:51
  129.7 0.2 fusion.26
  129.9 0.2 fusion.24
  130.1 40.7 %psum.7 = f32[2,128]{1,0:T(2,128)S(1)} all-reduce(f32[2,128]{1,0:T(2,128)S(1)} %fusion.24), channel_id=1, replica_groups=mesh['mp'=16,'dp'=32] {'mp'}, use_global_device_ids=true, to_apply=%region_3.4 | all-reduce | flops 256 | bytes 2048 | tf_op jit(solution)/shard_map/psum | solution.py:76
  170.8 0.6 dynamic-slice_multiply_fusion
  (13 shorter events, 0.1 us)
Async XLA Ops:
  6.5 2.1 %copy-start = (bf16[1,4,64,3584]{3,2,1,0:T(8,128)(2,1)S(1)}, bf16[1,4,64,3584]{3,2,1,0:T(8,128)(2,1)}, u32[]{:S(2)}) copy-start(bf16[1,4,64,3584]{3,2,1,0:T(8,128)(2,1)} %param.7) | copy-start | bytes 5505028
  6.5 88.6 %all-gather.3.cloned.1.call-start = ((), (), s32[]{:S(2)}) async-start(), calls=%async_computation | async-start | bytes 2162688 | tf_op jit(solution)/shard_map/all_gather | solution.py:68
  8.7 1.5 copy-start.2
  9.4 1.5 copy-start.1
  12.0 2.1 %copy-start.3 = (bf16[1,2,64,2048]{3,2,1,0:T(8,128)(2,1)S(1)}, bf16[1,2,64,2048]{3,2,1,0:T(8,128)(2,1)}, u32[]{:S(2)}) copy-start(bf16[1,2,64,2048]{3,2,1,0:T(8,128)(2,1)} %param.10) | copy-start | bytes 1572868
  13.9 0.7 copy-start.4
Sparse Core Ops, SparseCore 0:
  12.1 82.9 all-gather.2
where the time goes:
time: 178 us
  waiting for transfers between devices  80.2 us (45%)
  blocking collectives  40.7 us (23%)
  other arithmetic  23.7 us (13%)
  between operations  15.6 us (9%)
  matrix products  12.4 us (7%)
  local copies, waits for them, and re-layouts  5.74 us (3%)
    all_gather x1, waiting for transfers between devices, shards(): everyone = lax.all_gather(train_rows, 'dp', axis=0, tiled=True)  80.2 us
    psum x1, blocking collectives, shards(): summed = lax.psum(total, 'mp')  40.7 us
    another operation x3, other arithmetic, shards(): factor = jnp.linalg.cholesky(system)  12.4 us
    another operation x2, other arithmetic, shards(): solved = jax.scipy.linalg.cho_solve((factor, True), cross_terms.T).T  10.5 us
    dot_general x2, matrix products, inner_rows(): jnp.dot(first, second.T, precision=lax.Precision.HIGHEST, preferred_eleme...  7.97 us
    unnamed x12, local copies, waits for them, and re-layouts  3.69 us
  transfers between devices with their start and end apart: 1, of which 1 were waited for; matrix products, arithmetic and copies ran while one was open for 2% of the time, Pallas kernels for 0%

commit v1 on v0

v1 whole, which is shorter than its diff:
```python
import functools

import jax
import jax.numpy as jnp
from jax import lax
from jax.experimental import pallas as pl
from jax.experimental.pallas import tpu as pltpu
from jax.sharding import PartitionSpec as P

MESH = pl.DeviceIdType.MESH
R1 = 64
R2 = 64
RIDGE_SCALE = 0.1
LANES = 128
TILE = 8
PLANES = 4
SPOTS = 8
SLICE_ROWS = 4


def sign_table(salt, rows, table_ref):
    half = rows // 2
    row = lax.broadcasted_iota(jnp.int32, (LANES, LANES), 0)
    lane = lax.broadcasted_iota(jnp.int32, (LANES, LANES), 1)
    row = row + jnp.where(lane >= R1, half, 0)
    base = row * 73856093 + (lane & (R1 - 1)) * 19349663 + salt * 83492791
    scale = 1.0 / rows**0.5

    def chunk(step, carry):
        h = base + step * LANES * 73856093
        h = h ^ lax.shift_right_logical(h, 15)
        h = h * 1274126177
        h = h ^ lax.shift_right_logical(h, 13)
        h = h * 668265263
        bit = (lax.shift_right_logical(h, 16) ^ h) & 128
        signs = jnp.where(bit != 0, scale, -scale).astype(jnp.bfloat16)
        table_ref[pl.ds(pl.multiple_of(step * LANES, LANES), LANES), :] = signs
        return carry

    lax.fori_loop(0, half // LANES, chunk, 0, unroll=2)


def projected(tokens, table):
    half = table.shape[0]
    upper = jnp.dot(tokens[:, :half], table, preferred_element_type=jnp.float32)
    lower = jnp.dot(tokens[:, half:], table, preferred_element_type=jnp.float32)
    return upper[:, :R1] + lower[:, R1:]


def rows_by_columns(first, second):
    return lax.dot_general(
        first,
        second,
        (((1,), (1,)), ((), ())),
        precision=lax.Precision.HIGHEST,
        preferred_element_type=jnp.float32,
    )


def features(left, right, length):
    position = lax.broadcasted_iota(jnp.int32, left.shape, 0)
    left = jnp.where(position < length, left, 0.0)
    outer = lax.dot_general(
        left,
        right,
        (((0,), (0,)), ((), ())),
        precision=lax.Precision.HIGHEST,
        preferred_element_type=jnp.float32,
    )
    return jnp.concatenate([outer[: R1 // 2], outer[R1 // 2 :]], axis=1)


def solve(gram, rhs):
    total = gram.shape[0]
    lane = lax.broadcasted_iota(jnp.int32, (TILE, LANES), 1)
    blocks = total // TILE

    def spread(tile, column):
        return jnp.broadcast_to(tile[:, column : column + 1], (TILE, LANES))

    def down(tile, row):
        return jnp.broadcast_to(tile[row : row + 1, :], (TILE, LANES))

    def step(_, tiles):
        pivot, others = tiles[0], tiles[1:]
        columns = [spread(pivot, t) for t in range(TILE)]
        entry = {(k, t): down(columns[t], k) for t in range(TILE) for k in range(t + 1)}
        row = [jnp.where(lane == k, -1.0, jnp.where(lane < TILE, 0.0, down(pivot, k))) for k in range(TILE)]
        for t in range(TILE):
            inverse = 1.0 / entry[t, t]
            row[t] = row[t] * inverse
            scaled = {l: entry[t, l] * inverse for l in range(t + 1, TILE)}
            for k in range(TILE):
                if k == t:
                    continue
                factor = entry[t, k] if k > t else entry[k, t]
                row[k] = row[k] - factor * row[t]
                for l in range(t + 1, TILE):
                    if k < t or l >= k:
                        entry[k, l] = entry[k, l] - factor * scaled[l]
            for l in range(t + 1, TILE):
                entry[t, l] = scaled[l]
        changed = []
        for tile in others:
            terms = [spread(tile, k) * row[k] for k in range(TILE)]
            while len(terms) > 1:
                terms = [a + b for a, b in zip(terms[::2], terms[1::2])]
            tile = jnp.where(lane < TILE, 0.0, tile) - terms[0]
            changed.append(pltpu.roll(tile, LANES - TILE, 1))
        return (*changed[:-1], jnp.zeros_like(pivot), changed[-1])

    tiles = tuple(gram[TILE * b : TILE * (b + 1)] for b in range(blocks)) + (rhs,)
    return lax.fori_loop(0, blocks, step, tiles)[-1]


def kernel(
    salts, train_lengths, query_lengths, train_acts, train_grads, query_acts, query_grads, out_ref,
    acts, grads, table_in, table_out, train_send, query_send, train_recv, query_recv,
    gram_part, cross_part, gram_recv, cross_recv, gram_row, gram_full, score_send, score_recv, result_send, result_recv,
    load_sems, send_sems, recv_sems,
):
    dp, mp = lax.axis_index("dp"), lax.axis_index("mp")
    members, ckpts = lax.axis_size("dp"), lax.axis_size("mp")
    trains, queries = train_acts.shape[1], query_acts.shape[1]
    spot = lax.rem(dp, SPOTS)
    home = dp < SPOTS

    loads = [
        pltpu.make_async_copy(train_grads.at[0], grads.at[pl.ds(0, trains)], load_sems.at[0]),
        pltpu.make_async_copy(query_grads.at[0], grads.at[pl.ds(trains, queries)], load_sems.at[1]),
        pltpu.make_async_copy(train_acts.at[0], acts.at[pl.ds(0, trains)], load_sems.at[2]),
        pltpu.make_async_copy(query_acts.at[0], acts.at[pl.ds(trains, queries)], load_sems.at[3]),
    ]
    for load in loads:
        load.start()

    barrier = pltpu.get_barrier_semaphore()

    def greet_dp(peer):
        pl.semaphore_signal(barrier, inc=1, device_id={"dp": peer}, device_id_type=MESH)

    def greet_mp(peer):
        pl.semaphore_signal(barrier, inc=1, device_id={"mp": peer}, device_id_type=MESH)

    def send(phase, source, target, device):
        copy = pltpu.make_async_remote_copy(
            src_ref=source, dst_ref=target, send_sem=send_sems.at[phase], recv_sem=recv_sems.at[phase],
            device_id=device, device_id_type=MESH,
        )
        copy.start()

    def sent(phase, like):
        pltpu.make_async_copy(like, like, send_sems.at[phase]).wait()

    def received(phase, like):
        pltpu.make_async_copy(like, like, recv_sems.at[phase]).wait()

    @pl.when(home)
    def _():
        @pl.loop(1, members)
        def _(k):
            greet_dp(lax.rem(dp + k, members))

        @pl.loop(1, ckpts)
        def _(k):
            greet_mp(lax.rem(mp + k, ckpts))

    @pl.when(jnp.logical_not(home))
    def _():
        @pl.loop(0, SPOTS)
        def _(k):
            greet_dp(k)

    sign_table(salts[0, 1], grads.shape[2], table_out)
    sign_table(salts[0, 0], acts.shape[2], table_in)

    count, length = acts.shape[0], acts.shape[1]
    loads[0].wait()
    loads[1].wait()
    right = projected(grads[...].reshape(count * length, grads.shape[2]), table_out[...])
    loads[2].wait()
    loads[3].wait()
    left = projected(acts[...].reshape(count * length, acts.shape[2]), table_in[...])
    for e in range(count):
        tokens = slice(e * length, (e + 1) * length)
        tokens_used = train_lengths[e] if e < trains else query_lengths[e - trains]
        rows = features(left[tokens], right[tokens], tokens_used)
        rows = rows.reshape(SPOTS, SLICE_ROWS, LANES)
        if e < trains:
            for j in range(SLICE_ROWS):
                train_send[:, j // 2, (j % 2) * trains + e, :] = rows[:, j]
        else:
            for j in range(SLICE_ROWS):
                query_send[:, j * queries + e - trains, :] = rows[:, j]

    def spread_features(first):
        @pl.loop(first, SPOTS)
        def _(k):
            to = lax.rem(spot + k, SPOTS)
            send(0, train_send.at[to], train_recv.at[dp], {"dp": to})

        @pl.loop(first, SPOTS)
        def _(k):
            to = lax.rem(spot + k, SPOTS)
            send(1, query_send.at[to], query_recv.at[dp], {"dp": to})

    @pl.when(jnp.logical_not(home))
    def _():
        pl.semaphore_wait(barrier, SPOTS)
        spread_features(0)
        received(6, result_recv)
        out_ref[...] = result_recv[0:queries, 0 : out_ref.shape[1]]
        sent(0, train_send)
        sent(1, query_send)

    @pl.when(home)
    def _():
        pl.semaphore_wait(barrier, members - 1 + ckpts - 1)
        spread_features(1)
        train_recv[dp] = train_send[spot]
        query_recv[dp] = query_send[spot]
        others = pl.ds(0, members - 1)
        received(0, train_recv.at[others])

        low = lax.broadcasted_iota(jnp.int32, (members // 2, TILE, LANES), 1) < trains
        train_rows = []
        for j in range(SLICE_ROWS // 2):
            pairs = train_recv[:, j].reshape(members // 2, 2, TILE, LANES)
            even, odd = pairs[:, 0], pairs[:, 1]
            train_rows.append(jnp.where(low, even, pltpu.roll(odd, trains, 1)))
            train_rows.append(jnp.where(low, pltpu.roll(even, trains, 1), odd))
        train_rows = [rows.reshape(members * trains, LANES) for rows in train_rows]
        gram = rows_by_columns(train_rows[0], train_rows[0])
        for rows in train_rows[1:]:
            gram = gram + rows_by_columns(rows, rows)
        gram_part[...] = gram
        share = members * trains // SPOTS

        @pl.loop(1, SPOTS)
        def _(k):
            to = lax.rem(spot + k, SPOTS)
            send(2, gram_part.at[pl.ds(pl.multiple_of(to * share, share), share)], gram_recv.at[spot], {"dp": to})

        gram_recv[spot] = gram_part[pl.ds(pl.multiple_of(spot * share, share), share), :]

        received(1, query_recv.at[others])
        planes = query_recv[...].reshape(PLANES, SPOTS, TILE, LANES)
        position = lax.broadcasted_iota(jnp.int32, (SPOTS, TILE, LANES), 1) // queries
        cross = None
        for j in range(SLICE_ROWS):
            rows = jnp.zeros((SPOTS, TILE, LANES), jnp.float32)
            for plane in range(PLANES):
                shift = (queries * (plane - j)) % TILE
                moved = pltpu.roll(planes[plane], shift, 1) if shift else planes[plane]
                rows = jnp.where(position == plane, moved, rows)
            term = rows_by_columns(rows.reshape(SPOTS * TILE, LANES), train_rows[j])
            cross = term if cross is None else cross + term
        cross_part[...] = cross.reshape(SPOTS, TILE, LANES)

        @pl.loop(1, SPOTS)
        def _(k):
            to = lax.rem(spot + k, SPOTS)
            send(3, cross_part.at[to], cross_recv.at[spot], {"dp": to})

        cross_recv[spot] = cross_part[spot]

        rest = pl.ds(0, SPOTS - 1)
        received(2, gram_recv.at[rest])
        gram_row[...] = jnp.sum(gram_recv[...], axis=0)
        mine = pl.ds(pl.multiple_of(spot * share, share), share)

        @pl.loop(1, SPOTS)
        def _(k):
            send(4, gram_row, gram_full.at[mine], {"dp": lax.rem(spot + k, SPOTS)})

        gram_full[mine, :] = gram_row[...]
        received(3, cross_recv.at[rest])
        cross_terms = jnp.sum(cross_recv[...], axis=0)
        received(4, gram_full.at[pl.ds(0, share * (SPOTS - 1))])

        gram = gram_full[...]
        total = gram.shape[0]
        diagonal = lax.broadcasted_iota(jnp.int32, gram.shape, 0) == lax.broadcasted_iota(jnp.int32, gram.shape, 1)
        trace = jnp.sum(jnp.where(diagonal, gram, 0.0), axis=(0, 1), keepdims=True)
        ridge = RIDGE_SCALE * trace / total
        system = jnp.where(diagonal, gram + ridge, gram)
        solved = solve(system, cross_terms)

        score_send[...] = solved

        @pl.loop(1, ckpts)
        def _(k):
            send(5, score_send, score_recv.at[mp], {"mp": lax.rem(mp + k, ckpts)})

        score_recv[mp] = solved
        received(5, score_recv.at[pl.ds(0, ckpts - 1)])
        summed = jnp.sum(score_recv[...], axis=0) * (total / ckpts)
        width = out_ref.shape[1]
        summed = pltpu.roll(summed, lax.rem((ckpts - mp) * width, LANES), 1)
        for plane in range(1, PLANES):
            result_send[plane, 0:queries, :] = summed[plane * queries : (plane + 1) * queries]
            result_send[plane, queries:, :] = jnp.zeros((TILE - queries, LANES), jnp.float32)
            send(6, result_send.at[plane], result_recv, {"dp": plane * SPOTS + spot})
        out_ref[...] = summed[0:queries, 0:width]
        sent(0, train_send.at[rest])
        sent(1, query_send.at[rest])
        sent(2, gram_recv.at[rest])
        sent(3, cross_recv.at[rest])
        sent(4, gram_full.at[pl.ds(0, share * (SPOTS - 1))])
        sent(5, score_recv.at[pl.ds(0, ckpts - 1)])
        sent(6, result_send.at[pl.ds(0, PLANES - 1)])


def shards(train_acts, train_grads, query_acts, query_grads, train_lengths, query_lengths, proj_salts):
    _, trains, length, width = train_acts.shape
    queries, out_width = query_acts.shape[1], train_grads.shape[3]
    members, ckpts = lax.axis_size("dp"), lax.axis_size("mp")
    total = trains * members
    f32, bf16 = jnp.float32, jnp.bfloat16
    smem, hbm = pl.BlockSpec(memory_space=pltpu.SMEM), pl.BlockSpec(memory_space=pl.ANY)
    return pl.pallas_call(
        kernel,
        out_shape=jax.ShapeDtypeStruct((queries, total // ckpts), f32),
        in_specs=[smem] * 3 + [hbm] * 4,
        out_specs=pl.BlockSpec(memory_space=pltpu.VMEM),
        scratch_shapes=[
            pltpu.VMEM((trains + queries, length, width), bf16),
            pltpu.VMEM((trains + queries, length, out_width), bf16),
            pltpu.VMEM((width // 2, LANES), bf16),
            pltpu.VMEM((out_width // 2, LANES), bf16),
            pltpu.VMEM((SPOTS, SLICE_ROWS // 2, TILE, LANES), f32),
            pltpu.VMEM((SPOTS, TILE, LANES), f32),
            pltpu.VMEM((members, SLICE_ROWS // 2, TILE, LANES), f32),
            pltpu.VMEM((members, TILE, LANES), f32),
            pltpu.VMEM((total, LANES), f32),
            pltpu.VMEM((SPOTS, TILE, LANES), f32),
            pltpu.VMEM((SPOTS, total // SPOTS, LANES), f32),
            pltpu.VMEM((SPOTS, TILE, LANES), f32),
            pltpu.VMEM((total // SPOTS, LANES), f32),
            pltpu.VMEM((total, LANES), f32),
            pltpu.VMEM((TILE, LANES), f32),
            pltpu.VMEM((ckpts, TILE, LANES), f32),
            pltpu.VMEM((PLANES, TILE, LANES), f32),
            pltpu.VMEM((TILE, LANES), f32),
            pltpu.SemaphoreType.DMA((4,)),
            pltpu.SemaphoreType.DMA((7,)),
            pltpu.SemaphoreType.DMA((7,)),
        ],
        compiler_params=pltpu.CompilerParams(
            collective_id=0, has_side_effects=True, vmem_limit_bytes=48 * 1024 * 1024
        ),
    )(proj_salts, train_lengths, query_lengths, train_acts, train_grads, query_acts, query_grads)


def solution(mesh):
    placed = (
        P("mp", "dp", None, None),
        P("mp", "dp", None, None),
        P("mp", "dp", None, None),
        P("mp", "dp", None, None),
        P("dp"),
        P("dp"),
        P("mp", None),
    )
    return jax.shard_map(shards, mesh=mesh, in_specs=placed, out_specs=P("dp", "mp"), check_vma=False)
```

time: 178 us -> 63.5 us (0.36)
  the two profiles are of different devices: /device:TPU:2 before, /device:TPU:1 now
where the time goes in v1:
time: 63.5 us; the launch traced here: 63.2 us
  Pallas kernels  55.8 us (88%)
  local copies, waits for them, and re-layouts  7.47 us (12%)
    pallas_call x1, Pallas kernels, shards(): pl.pallas_call(kernel, out_shape=jax.ShapeDtypeStruct((queries, total //...  55.8 us
    unnamed x15, local copies, waits for them, and re-layouts  7.47 us

profile of v1, /device:TPU:1, one launch (start us, length us, event | category | flops | bytes accessed | tf_op | source)
XLA Modules:
  0.0 63.2 jit_solution(1304508342421971504)
XLA Ops:
  0.0 0.0 copy-start
  0.0 1.5 %copy-done = bf16[1,4,64,3584]{3,2,1,0:T(8,128)(2,1)S(1)} copy-done((bf16[1,4,64,3584]{3,2,1,0:T(8,128)(2,1)S(1)}, bf16[1,4,64,3584]{3,2,1,0:T(8,128)(2,1)}, u32[]{:S(2)}) %copy-start) | copy-done | bytes 1835032
  1.5 0.0 copy-start.1
  1.5 1.2 %copy-done.1 = bf16[1,4,64,2048]{3,2,1,0:T(8,128)(2,1)S(1)} copy-done((bf16[1,4,64,2048]{3,2,1,0:T(8,128)(2,1)S(1)}, bf16[1,4,64,2048]{3,2,1,0:T(8,128)(2,1)}, u32[]{:S(2)}) %copy-start.1) | copy-done | bytes 1048600
  2.7 0.0 copy-start.2
  2.7 1.2 %copy-done.2 = bf16[1,2,64,3584]{3,2,1,0:T(8,128)(2,1)S(1)} copy-done((bf16[1,2,64,3584]{3,2,1,0:T(8,128)(2,1)S(1)}, bf16[1,2,64,3584]{3,2,1,0:T(8,128)(2,1)}, u32[]{:S(2)}) %copy-start.2) | copy-done | bytes 917528
  3.9 0.0 copy-start.3
  3.9 1.0 %copy-done.3 = bf16[1,2,64,2048]{3,2,1,0:T(8,128)(2,1)S(1)} copy-done((bf16[1,2,64,2048]{3,2,1,0:T(8,128)(2,1)S(1)}, bf16[1,2,64,2048]{3,2,1,0:T(8,128)(2,1)}, u32[]{:S(2)}) %copy-start.3) | copy-done | bytes 524312
  4.9 0.0 copy-start.4
  4.9 0.7 %copy-done.4 = s32[1,2]{1,0:T(1,128)S(1)} copy-done((s32[1,2]{1,0:T(1,128)S(1)}, s32[1,2]{1,0:T(1,128)}, u32[]{:S(2)}) %copy-start.4) | copy-done | bytes 32
  5.6 0.0 copy-start.5
  5.6 0.7 %copy-done.5 = s32[4]{0:T(128)S(1)} copy-done((s32[4]{0:T(128)S(1)}, s32[4]{0:T(128)}, u32[]{:S(2)}) %copy-start.5) | copy-done | bytes 40
  6.3 0.0 copy-start.6
  6.3 0.7 %copy-done.6 = s32[2]{0:T(128)S(1)} copy-done((s32[2]{0:T(128)S(1)}, s32[2]{0:T(128)}, u32[]{:S(2)}) %copy-start.6) | copy-done | bytes 32
  6.9 55.8 %shard_map.73 = f32[2,8]{1,0:T(2,128)S(1)} custom-call(s32[1,2]{1,0:T(1,128)S(1)} %copy-done.4, s32[4]{0:T(128)S(1)} %copy-done.5, s32[2]{0:T(128)S(1)} %copy-done.6, bf16[1,4,64,3584]{3,2,1,0:T(8,128)(2,1)S(1)} %copy-done, bf16[1,4,64,2048]{3,2,1,0:T(8,128)(2,1)S(1)} %copy-done.1, bf16[1,2,64,3584]{3,2,1,0:T(8,128)(2,1)S(1)} %copy-done.2, ...), custom_call_target="tpu_custom_call" | custom-call | tf_op jit(solution)/shard_map/pallas_call | solution.py:321
  62.7 0.6 copy.9
Async XLA Ops:
  0.0 1.5 %copy-start = (bf16[1,4,64,3584]{3,2,1,0:T(8,128)(2,1)S(1)}, bf16[1,4,64,3584]{3,2,1,0:T(8,128)(2,1)}, u32[]{:S(2)}) copy-start(bf16[1,4,64,3584]{3,2,1,0:T(8,128)(2,1)} %train_acts.1) | copy-start | bytes 5505028
  1.5 1.2 %copy-start.1 = (bf16[1,4,64,2048]{3,2,1,0:T(8,128)(2,1)S(1)}, bf16[1,4,64,2048]{3,2,1,0:T(8,128)(2,1)}, u32[]{:S(2)}) copy-start(bf16[1,4,64,2048]{3,2,1,0:T(8,128)(2,1)} %train_grads.1) | copy-start | bytes 3145732
  2.7 1.2 %copy-start.2 = (bf16[1,2,64,3584]{3,2,1,0:T(8,128)(2,1)S(1)}, bf16[1,2,64,3584]{3,2,1,0:T(8,128)(2,1)}, u32[]{:S(2)}) copy-start(bf16[1,2,64,3584]{3,2,1,0:T(8,128)(2,1)} %query_acts.1) | copy-start | bytes 2752516
  3.9 1.0 %copy-start.3 = (bf16[1,2,64,2048]{3,2,1,0:T(8,128)(2,1)S(1)}, bf16[1,2,64,2048]{3,2,1,0:T(8,128)(2,1)}, u32[]{:S(2)}) copy-start(bf16[1,2,64,2048]{3,2,1,0:T(8,128)(2,1)} %query_grads.1) | copy-start | bytes 1572868
  4.9 0.7 %copy-start.4 = (s32[1,2]{1,0:T(1,128)S(1)}, s32[1,2]{1,0:T(1,128)}, u32[]{:S(2)}) copy-start(s32[1,2]{1,0:T(1,128)} %salts.1) | copy-start | bytes 28
  5.6 0.7 %copy-start.5 = (s32[4]{0:T(128)S(1)}, s32[4]{0:T(128)}, u32[]{:S(2)}) copy-start(s32[4]{0:T(128)} %train_lengths.1) | copy-start | bytes 52
  6.3 0.7 %copy-start.6 = (s32[2]{0:T(128)S(1)}, s32[2]{0:T(128)}, u32[]{:S(2)}) copy-start(s32[2]{0:T(128)} %query_lengths.1) | copy-start | bytes 28

commit v2 on v1

--- a/solution.py
+++ b/solution.py
@@ -117,7 +117,7 @@
     salts, train_lengths, query_lengths, train_acts, train_grads, query_acts, query_grads, out_ref,
     acts, grads, table_in, table_out, train_send, query_send, train_recv, query_recv,
     gram_part, cross_part, gram_recv, cross_recv, gram_row, gram_full, score_send, score_recv, result_send, result_recv,
-    load_sems, send_sems, recv_sems,
+    salts_here, train_lengths_here, query_lengths_here, load_sems, send_sems, recv_sems,
 ):
     dp, mp = lax.axis_index("dp"), lax.axis_index("mp")
     members, ckpts = lax.axis_size("dp"), lax.axis_size("mp")
@@ -125,13 +125,18 @@
     spot = lax.rem(dp, SPOTS)
     home = dp < SPOTS
 
+    small = [
+        pltpu.make_async_copy(salts, salts_here, load_sems.at[4]),
+        pltpu.make_async_copy(train_lengths, train_lengths_here, load_sems.at[5]),
+        pltpu.make_async_copy(query_lengths, query_lengths_here, load_sems.at[6]),
+    ]
     loads = [
         pltpu.make_async_copy(train_grads.at[0], grads.at[pl.ds(0, trains)], load_sems.at[0]),
         pltpu.make_async_copy(query_grads.at[0], grads.at[pl.ds(trains, queries)], load_sems.at[1]),
         pltpu.make_async_copy(train_acts.at[0], acts.at[pl.ds(0, trains)], load_sems.at[2]),
         pltpu.make_async_copy(query_acts.at[0], acts.at[pl.ds(trains, queries)], load_sems.at[3]),
     ]
-    for load in loads:
+    for load in small + loads:
         load.start()
 
     barrier = pltpu.get_barrier_semaphore()
@@ -171,8 +176,9 @@
         def _(k):
             greet_dp(k)
 
-    sign_table(salts[0, 1], grads.shape[2], table_out)
-    sign_table(salts[0, 0], acts.shape[2], table_in)
+    small[0].wait()
+    sign_table(salts_here[0, 1], grads.shape[2], table_out)
+    sign_table(salts_here[0, 0], acts.shape[2], table_in)
 
     count, length = acts.shape[0], acts.shape[1]
     loads[0].wait()
@@ -181,9 +187,11 @@
     loads[2].wait()
     loads[3].wait()
     left = projected(acts[...].reshape(count * length, acts.shape[2]), table_in[...])
+    small[1].wait()
+    small[2].wait()
     for e in range(count):
         tokens = slice(e * length, (e + 1) * length)
-        tokens_used = train_lengths[e] if e < trains else query_lengths[e - trains]
+        tokens_used = train_lengths_here[e] if e < trains else query_lengths_here[e - trains]
         rows = features(left[tokens], right[tokens], tokens_used)
         rows = rows.reshape(SPOTS, SLICE_ROWS, LANES)
         if e < trains:
@@ -317,11 +325,11 @@
     members, ckpts = lax.axis_size("dp"), lax.axis_size("mp")
     total = trains * members
     f32, bf16 = jnp.float32, jnp.bfloat16
-    smem, hbm = pl.BlockSpec(memory_space=pltpu.SMEM), pl.BlockSpec(memory_space=pl.ANY)
+    i32 = jnp.int32
     return pl.pallas_call(
         kernel,
         out_shape=jax.ShapeDtypeStruct((queries, total // ckpts), f32),
-        in_specs=[smem] * 3 + [hbm] * 4,
+        in_specs=[pl.BlockSpec(memory_space=pltpu.HBM)] * 7,
         out_specs=pl.BlockSpec(memory_space=pltpu.VMEM),
         scratch_shapes=[
             pltpu.VMEM((trains + queries, length, width), bf16),
@@ -342,12 +350,15 @@
             pltpu.VMEM((ckpts, TILE, LANES), f32),
             pltpu.VMEM((PLANES, TILE, LANES), f32),
             pltpu.VMEM((TILE, LANES), f32),
-            pltpu.SemaphoreType.DMA((4,)),
+            pltpu.SMEM((1, 2), i32),
+            pltpu.SMEM((trains,), i32),
+            pltpu.SMEM((queries,), i32),
+            pltpu.SemaphoreType.DMA((7,)),
             pltpu.SemaphoreType.DMA((7,)),
             pltpu.SemaphoreType.DMA((7,)),
         ],
         compiler_params=pltpu.CompilerParams(
-            collective_id=0, has_side_effects=True, vmem_limit_bytes=48 * 1024 * 1024
+            collective_id=0, has_side_effects=True, vmem_limit_bytes=64 * 1024 * 1024
         ),
     )(proj_salts, train_lengths, query_lengths, train_acts, train_grads, query_acts, query_grads)
 

time: 63.5 us -> 57.4 us (0.904)
  local copies, waits for them, and re-layouts: 7.47 us -> 1.24 us
    unnamed x15 -> x1, local copies, waits for them, and re-layouts: 7.47 us -> 1.24 us
where the time goes in v2:
time: 57.4 us; the launch traced here: 57.3 us
  Pallas kernels  56 us (98%)
  local copies, waits for them, and re-layouts  1.24 us (2%)
    pallas_call x1, Pallas kernels, shards(): pl.pallas_call(kernel, out_shape=jax.ShapeDtypeStruct((queries, total //...  56 us
    unnamed x1, local copies, waits for them, and re-layouts  1.24 us

profile of v2, /device:TPU:1, one launch (start us, length us, event | category | flops | bytes accessed | tf_op | source)
XLA Modules:
  0.0 57.3 jit_solution(1667582119988361789)
XLA Ops:
  0.0 56.0 %shard_map.73 = f32[2,8]{1,0:T(2,128)} custom-call(s32[1,2]{1,0:T(1,128)} %salts.1, s32[4]{0:T(128)} %train_lengths.1, s32[2]{0:T(128)} %query_lengths.1, bf16[1,4,64,3584]{3,2,1,0:T(8,128)(2,1)} %train_acts.1, bf16[1,4,64,2048]{3,2,1,0:T(8,128)(2,1)} %train_grads.1, bf16[1,2,64,3584]{3,2,1,0:T(8,128)(2,1)} %query_acts.1, bf16[1,2,64,2048]{3,2,1,0:T(8,128)(2,1)} %query_grads.1), custom_call_target="tpu_custom_call" | custom-call | tf_op jit(solution)/shard_map/pallas_call | solution.py:329
  56.1 1.2 %copy.9 = f32[2,8]{1,0:T(2,128)} copy(f32[2,8]{1,0:T(2,128)} %shard_map.73) | data formatting | bytes 128

commit v3 on v2

--- a/solution.py
+++ b/solution.py
@@ -15,6 +15,7 @@
 TILE = 8
 PLANES = 4
 SPOTS = 8
+PIVOTS = 16
 SLICE_ROWS = 4
 
 
@@ -72,8 +73,9 @@
 
 def solve(gram, rhs):
     total = gram.shape[0]
+    high = PIVOTS // TILE
+    sublane = lax.broadcasted_iota(jnp.int32, (TILE, LANES), 0)
     lane = lax.broadcasted_iota(jnp.int32, (TILE, LANES), 1)
-    blocks = total // TILE
 
     def spread(tile, column):
         return jnp.broadcast_to(tile[:, column : column + 1], (TILE, LANES))
@@ -81,36 +83,34 @@
     def down(tile, row):
         return jnp.broadcast_to(tile[row : row + 1, :], (TILE, LANES))
 
-    def step(_, tiles):
-        pivot, others = tiles[0], tiles[1:]
-        columns = [spread(pivot, t) for t in range(TILE)]
-        entry = {(k, t): down(columns[t], k) for t in range(TILE) for k in range(t + 1)}
-        row = [jnp.where(lane == k, -1.0, jnp.where(lane < TILE, 0.0, down(pivot, k))) for k in range(TILE)]
-        for t in range(TILE):
-            inverse = 1.0 / entry[t, t]
-            row[t] = row[t] * inverse
-            scaled = {l: entry[t, l] * inverse for l in range(t + 1, TILE)}
-            for k in range(TILE):
-                if k == t:
-                    continue
-                factor = entry[t, k] if k > t else entry[k, t]
-                row[k] = row[k] - factor * row[t]
-                for l in range(t + 1, TILE):
-                    if k < t or l >= k:
-                        entry[k, l] = entry[k, l] - factor * scaled[l]
-            for l in range(t + 1, TILE):
-                entry[t, l] = scaled[l]
-        changed = []
-        for tile in others:
-            terms = [spread(tile, k) * row[k] for k in range(TILE)]
+    tiles = [gram[TILE * b : TILE * (b + 1)] for b in range(total // TILE)] + [rhs]
+    for start in range(0, total, PIVOTS):
+        first = start // TILE
+        inside = (lane >= start) & (lane < start + PIVOTS)
+        block = tiles[first : first + high]
+        columns = [[spread(tile, start + t) for tile in block] for t in range(PIVOTS)]
+        rows = [
+            jnp.where(inside, jnp.where(lane - start == sublane + TILE * g, -1.0, 0.0), block[g]) for g in range(high)
+        ]
+        for t in range(PIVOTS):
+            g, r = t // TILE, t % TILE
+            here = sublane == r
+            inverse = 1.0 / down(columns[t][g], r)
+            pivot_row = down(rows[g], r) * inverse
+            rows = [rows[i] - columns[t][i] * pivot_row for i in range(high)]
+            rows[g] = jnp.where(here, pivot_row, rows[g])
+            for c in range(t + 1, PIVOTS):
+                scaled = down(columns[c][g], r) * inverse
+                column = [columns[c][i] - columns[t][i] * scaled for i in range(high)]
+                column[g] = jnp.where(here, scaled, column[g])
+                columns[c] = column
+        pivots = [down(rows[t // TILE], t % TILE) for t in range(PIVOTS)]
+        for i in range(first + high, len(tiles)):
+            terms = [spread(tiles[i], start + t) * pivots[t] for t in range(PIVOTS)]
             while len(terms) > 1:
                 terms = [a + b for a, b in zip(terms[::2], terms[1::2])]
-            tile = jnp.where(lane < TILE, 0.0, tile) - terms[0]
-            changed.append(pltpu.roll(tile, LANES - TILE, 1))
-        return (*changed[:-1], jnp.zeros_like(pivot), changed[-1])
-
-    tiles = tuple(gram[TILE * b : TILE * (b + 1)] for b in range(blocks)) + (rhs,)
-    return lax.fori_loop(0, blocks, step, tiles)[-1]
+            tiles[i] = jnp.where(inside, 0.0, tiles[i]) - terms[0]
+    return tiles[-1]
 
 
 def kernel(

time: 57.4 us -> 51.9 us (0.904)
  Pallas kernels: 56 us -> 50.6 us
    pallas_call x1, Pallas kernels: 56 us -> 50.6 us  [shards(): pl.pallas_call(kernel, out_shape=jax.ShapeDtypeStruct((queries, total //...]
where the time goes in v3:
time: 51.9 us; the launch traced here: 51.8 us
  Pallas kernels  50.6 us (97%)
  local copies, waits for them, and re-layouts  1.24 us (2%)
    pallas_call x1, Pallas kernels, shards(): pl.pallas_call(kernel, out_shape=jax.ShapeDtypeStruct((queries, total //...  50.6 us
    unnamed x1, local copies, waits for them, and re-layouts  1.24 us

profile of v3, /device:TPU:1, one launch (start us, length us, event | category | flops | bytes accessed | tf_op | source)
XLA Modules:
  0.0 51.8 jit_solution(16077193444097526515)
XLA Ops:
  0.0 50.6 %shard_map.73 = f32[2,8]{1,0:T(2,128)} custom-call(s32[1,2]{1,0:T(1,128)} %salts.1, s32[4]{0:T(128)} %train_lengths.1, s32[2]{0:T(128)} %query_lengths.1, bf16[1,4,64,3584]{3,2,1,0:T(8,128)(2,1)} %train_acts.1, bf16[1,4,64,2048]{3,2,1,0:T(8,128)(2,1)} %train_grads.1, bf16[1,2,64,3584]{3,2,1,0:T(8,128)(2,1)} %query_acts.1, bf16[1,2,64,2048]{3,2,1,0:T(8,128)(2,1)} %query_grads.1), custom_call_target="tpu_custom_call" | custom-call | tf_op jit(solution)/shard_map/pallas_call | solution.py:329
  50.6 1.2 %copy.9 = f32[2,8]{1,0:T(2,128)} copy(f32[2,8]{1,0:T(2,128)} %shard_map.73) | data formatting | bytes 128

commit v4 on v3

--- a/solution.py
+++ b/solution.py
@@ -14,6 +14,7 @@
 LANES = 128
 TILE = 8
 PLANES = 4
+FIRST_PLANE = 7
 SPOTS = 8
 PIVOTS = 16
 SLICE_ROWS = 4
@@ -48,12 +49,17 @@
     return upper[:, :R1] + lower[:, R1:]
 
 
-def rows_by_columns(first, second):
+def halves(values):
+    high = values.astype(jnp.bfloat16)
+    return high, (values - high.astype(jnp.float32)).astype(jnp.bfloat16)
+
+
+def product(first, second, axis):
+    (first_high, first_low), (second_high, second_low) = first, second
     return lax.dot_general(
-        first,
-        second,
-        (((1,), (1,)), ((), ())),
-        precision=lax.Precision.HIGHEST,
+        jnp.concatenate([first_high, first_high, first_low], axis=axis),
+        jnp.concatenate([second_high, second_low, second_high], axis=axis),
+        (((axis,), (axis,)), ((), ())),
         preferred_element_type=jnp.float32,
     )
 
@@ -61,13 +67,7 @@
 def features(left, right, length):
     position = lax.broadcasted_iota(jnp.int32, left.shape, 0)
     left = jnp.where(position < length, left, 0.0)
-    outer = lax.dot_general(
-        left,
-        right,
-        (((0,), (0,)), ((), ())),
-        precision=lax.Precision.HIGHEST,
-        preferred_element_type=jnp.float32,
-    )
+    outer = product(halves(left), halves(right), 0)
     return jnp.concatenate([outer[: R1 // 2], outer[R1 // 2 :]], axis=1)
 
 
@@ -115,7 +115,7 @@
 
 def kernel(
     salts, train_lengths, query_lengths, train_acts, train_grads, query_acts, query_grads, out_ref,
-    acts, grads, table_in, table_out, train_send, query_send, train_recv, query_recv,
+    acts, grads, table_in, table_out, train_send, query_send, train_recv, query_recv, train_high, train_low,
     gram_part, cross_part, gram_recv, cross_recv, gram_row, gram_full, score_send, score_recv, result_send, result_recv,
     salts_here, train_lengths_here, query_lengths_here, load_sems, send_sems, recv_sems,
 ):
@@ -132,11 +132,11 @@
     ]
     loads = [
         pltpu.make_async_copy(train_grads.at[0], grads.at[pl.ds(0, trains)], load_sems.at[0]),
-        pltpu.make_async_copy(query_grads.at[0], grads.at[pl.ds(trains, queries)], load_sems.at[1]),
-        pltpu.make_async_copy(train_acts.at[0], acts.at[pl.ds(0, trains)], load_sems.at[2]),
+        pltpu.make_async_copy(train_acts.at[0], acts.at[pl.ds(0, trains)], load_sems.at[1]),
+        pltpu.make_async_copy(query_grads.at[0], grads.at[pl.ds(trains, queries)], load_sems.at[2]),
         pltpu.make_async_copy(query_acts.at[0], acts.at[pl.ds(trains, queries)], load_sems.at[3]),
     ]
-    for load in small + loads:
+    for load in small + loads[:2]:
         load.start()
 
     barrier = pltpu.get_barrier_semaphore()
@@ -147,10 +147,10 @@
     def greet_mp(peer):
         pl.semaphore_signal(barrier, inc=1, device_id={"mp": peer}, device_id_type=MESH)
 
-    def send(phase, source, target, device):
+    def send(phase, source, target, device, arrival=None):
         copy = pltpu.make_async_remote_copy(
-            src_ref=source, dst_ref=target, send_sem=send_sems.at[phase], recv_sem=recv_sems.at[phase],
-            device_id=device, device_id_type=MESH,
+            src_ref=source, dst_ref=target, send_sem=send_sems.at[phase],
+            recv_sem=recv_sems.at[phase if arrival is None else arrival], device_id=device, device_id_type=MESH,
         )
         copy.start()
 
@@ -180,68 +180,85 @@
     sign_table(salts_here[0, 1], grads.shape[2], table_out)
     sign_table(salts_here[0, 0], acts.shape[2], table_in)
 
-    count, length = acts.shape[0], acts.shape[1]
-    loads[0].wait()
-    loads[1].wait()
-    right = projected(grads[...].reshape(count * length, grads.shape[2]), table_out[...])
-    loads[2].wait()
-    loads[3].wait()
-    left = projected(acts[...].reshape(count * length, acts.shape[2]), table_in[...])
+    length = acts.shape[1]
+
+    def example_features(first, count):
+        some = pl.ds(first, count)
+        right = projected(grads[some].reshape(count * length, grads.shape[2]), table_out[...])
+        loads[1 if first == 0 else 3].wait()
+        left = projected(acts[some].reshape(count * length, acts.shape[2]), table_in[...])
+        for e in range(count):
+            tokens = slice(e * length, (e + 1) * length)
+            used = train_lengths_here[e] if first == 0 else query_lengths_here[e]
+            yield e, features(left[tokens], right[tokens], used).reshape(SPOTS, SLICE_ROWS, LANES)
+
     small[1].wait()
     small[2].wait()
-    for e in range(count):
-        tokens = slice(e * length, (e + 1) * length)
-        tokens_used = train_lengths_here[e] if e < trains else query_lengths_here[e - trains]
-        rows = features(left[tokens], right[tokens], tokens_used)
-        rows = rows.reshape(SPOTS, SLICE_ROWS, LANES)
-        if e < trains:
-            for j in range(SLICE_ROWS):
-                train_send[:, j // 2, (j % 2) * trains + e, :] = rows[:, j]
-        else:
-            for j in range(SLICE_ROWS):
-                query_send[:, j * queries + e - trains, :] = rows[:, j]
-
-    def spread_features(first):
+    loads[0].wait()
+    loads[2].start()
+    loads[3].start()
+    for e, rows in example_features(0, trains):
+        for j in range(SLICE_ROWS):
+            train_send[:, j // 2, (j % 2) * trains + e, :] = rows[:, j]
+
+    plane_here = dp // SPOTS
+
+    def send_trains(first):
         @pl.loop(first, SPOTS)
         def _(k):
             to = lax.rem(spot + k, SPOTS)
-            send(0, train_send.at[to], train_recv.at[dp], {"dp": to})
-
+            send(0, train_send.at[to], train_recv.at[dp], {"dp": to}, arrival=FIRST_PLANE + plane_here)
+
+    def send_queries(first):
         @pl.loop(first, SPOTS)
         def _(k):
             to = lax.rem(spot + k, SPOTS)
             send(1, query_send.at[to], query_recv.at[dp], {"dp": to})
+
+    def query_features():
+        loads[2].wait()
+        for e, rows in example_features(trains, queries):
+            for j in range(SLICE_ROWS):
+                query_send[:, j * queries + e, :] = rows[:, j]
 
     @pl.when(jnp.logical_not(home))
     def _():
         pl.semaphore_wait(barrier, SPOTS)
-        spread_features(0)
+        send_trains(0)
+        query_features()
+        sent(0, train_send)
+        send_queries(0)
         received(6, result_recv)
         out_ref[...] = result_recv[0:queries, 0 : out_ref.shape[1]]
-        sent(0, train_send)
         sent(1, query_send)
 
     @pl.when(home)
     def _():
+        query_features()
         pl.semaphore_wait(barrier, members - 1 + ckpts - 1)
-        spread_features(1)
+        send_trains(1)
+        send_queries(1)
         train_recv[dp] = train_send[spot]
         query_recv[dp] = query_send[spot]
-        others = pl.ds(0, members - 1)
-        received(0, train_recv.at[others])
-
-        low = lax.broadcasted_iota(jnp.int32, (members // 2, TILE, LANES), 1) < trains
-        train_rows = []
-        for j in range(SLICE_ROWS // 2):
-            pairs = train_recv[:, j].reshape(members // 2, 2, TILE, LANES)
-            even, odd = pairs[:, 0], pairs[:, 1]
-            train_rows.append(jnp.where(low, even, pltpu.roll(odd, trains, 1)))
-            train_rows.append(jnp.where(low, pltpu.roll(even, trains, 1), odd))
-        train_rows = [rows.reshape(members * trains, LANES) for rows in train_rows]
-        gram = rows_by_columns(train_rows[0], train_rows[0])
-        for rows in train_rows[1:]:
-            gram = gram + rows_by_columns(rows, rows)
-        gram_part[...] = gram
+
+        low = lax.broadcasted_iota(jnp.int32, (SPOTS // 2, TILE, LANES), 1) < trains
+        height = SPOTS * trains
+        for plane in (0, 1, 3, 2):
+            arrived = SPOTS if plane else SPOTS - 1
+            received(FIRST_PLANE + plane, train_recv.at[pl.ds(0, arrived)])
+            for j in range(SLICE_ROWS):
+                pairs = train_recv[plane * SPOTS : (plane + 1) * SPOTS, j // 2]
+                pairs = pairs.reshape(SPOTS // 2, 2, TILE, LANES)
+                even, odd = pairs[:, 0], pairs[:, 1]
+                if j % 2 == 0:
+                    rows = jnp.where(low, even, pltpu.roll(odd, trains, 1))
+                else:
+                    rows = jnp.where(low, pltpu.roll(even, trains, 1), odd)
+                high_part, low_part = halves(rows.reshape(height, LANES))
+                train_high[plane * height : (plane + 1) * height, j * LANES : (j + 1) * LANES] = high_part
+                train_low[plane * height : (plane + 1) * height, j * LANES : (j + 1) * LANES] = low_part
+        train_halves = train_high[...], train_low[...]
+        gram_part[...] = product(train_halves, train_halves, 1)
         share = members * trains // SPOTS
 
         @pl.loop(1, SPOTS)
@@ -251,18 +268,29 @@
 
         gram_recv[spot] = gram_part[pl.ds(pl.multiple_of(spot * share, share), share), :]
 
-        received(1, query_recv.at[others])
+        rest = pl.ds(0, SPOTS - 1)
+        received(2, gram_recv.at[rest])
+        gram_row[...] = jnp.sum(gram_recv[...], axis=0)
+        mine = pl.ds(pl.multiple_of(spot * share, share), share)
+
+        @pl.loop(1, SPOTS)
+        def _(k):
+            send(4, gram_row, gram_full.at[mine], {"dp": lax.rem(spot + k, SPOTS)})
+
+        gram_full[mine, :] = gram_row[...]
+
+        received(1, query_recv.at[pl.ds(0, members - 1)])
         planes = query_recv[...].reshape(PLANES, SPOTS, TILE, LANES)
         position = lax.broadcasted_iota(jnp.int32, (SPOTS, TILE, LANES), 1) // queries
-        cross = None
+        slices = []
         for j in range(SLICE_ROWS):
             rows = jnp.zeros((SPOTS, TILE, LANES), jnp.float32)
             for plane in range(PLANES):
                 shift = (queries * (plane - j)) % TILE
                 moved = pltpu.roll(planes[plane], shift, 1) if shift else planes[plane]
                 rows = jnp.where(position == plane, moved, rows)
-            term = rows_by_columns(rows.reshape(SPOTS * TILE, LANES), train_rows[j])
-            cross = term if cross is None else cross + term
+            slices.append(rows.reshape(SPOTS * TILE, LANES))
+        cross = product(halves(jnp.concatenate(slices, axis=1)), (train_high[...], train_low[...]), 1)
         cross_part[...] = cross.reshape(SPOTS, TILE, LANES)
 
         @pl.loop(1, SPOTS)
@@ -272,16 +300,6 @@
 
         cross_recv[spot] = cross_part[spot]
 
-        rest = pl.ds(0, SPOTS - 1)
-        received(2, gram_recv.at[rest])
-        gram_row[...] = jnp.sum(gram_recv[...], axis=0)
-        mine = pl.ds(pl.multiple_of(spot * share, share), share)
-
-        @pl.loop(1, SPOTS)
-        def _(k):
-            send(4, gram_row, gram_full.at[mine], {"dp": lax.rem(spot + k, SPOTS)})
-
-        gram_full[mine, :] = gram_row[...]
         received(3, cross_recv.at[rest])
         cross_terms = jnp.sum(cross_recv[...], axis=0)
         received(4, gram_full.at[pl.ds(0, share * (SPOTS - 1))])
@@ -340,6 +358,8 @@
             pltpu.VMEM((SPOTS, TILE, LANES), f32),
             pltpu.VMEM((members, SLICE_ROWS // 2, TILE, LANES), f32),
             pltpu.VMEM((members, TILE, LANES), f32),
+            pltpu.VMEM((total, SLICE_ROWS * LANES), bf16),
+            pltpu.VMEM((total, SLICE_ROWS * LANES), bf16),
             pltpu.VMEM((total, LANES), f32),
             pltpu.VMEM((SPOTS, TILE, LANES), f32),
             pltpu.VMEM((SPOTS, total // SPOTS, LANES), f32),
@@ -354,8 +374,8 @@
             pltpu.SMEM((trains,), i32),
             pltpu.SMEM((queries,), i32),
             pltpu.SemaphoreType.DMA((7,)),
-            pltpu.SemaphoreType.DMA((7,)),
-            pltpu.SemaphoreType.DMA((7,)),
+            pltpu.SemaphoreType.DMA((FIRST_PLANE,)),
+            pltpu.SemaphoreType.DMA((FIRST_PLANE + PLANES,)),
         ],
         compiler_params=pltpu.CompilerParams(
             collective_id=0, has_side_effects=True, vmem_limit_bytes=64 * 1024 * 1024

time: 51.9 us -> 50.1 us (0.965)
  Pallas kernels: 50.6 us -> 48.7 us
    pallas_call x1, Pallas kernels: 50.6 us -> 48.7 us  [shards(): pl.pallas_call(kernel, out_shape=jax.ShapeDtypeStruct((queries, total //...]
where the time goes in v4:
time: 50.1 us; the launch traced here: 50 us
  Pallas kernels  48.7 us (97%)
  local copies, waits for them, and re-layouts  1.24 us (2%)
    pallas_call x1, Pallas kernels, shards(): pl.pallas_call(kernel, out_shape=jax.ShapeDtypeStruct((queries, total //...  48.7 us
    unnamed x1, local copies, waits for them, and re-layouts  1.24 us

profile of v4, /device:TPU:1, one launch (start us, length us, event | category | flops | bytes accessed | tf_op | source)
XLA Modules:
  0.0 50.0 jit_solution(16064511226157339895)
XLA Ops:
  0.0 48.7 %shard_map.73 = f32[2,8]{1,0:T(2,128)} custom-call(s32[1,2]{1,0:T(1,128)} %salts.1, s32[4]{0:T(128)} %train_lengths.1, s32[2]{0:T(128)} %query_lengths.1, bf16[1,4,64,3584]{3,2,1,0:T(8,128)(2,1)} %train_acts.1, bf16[1,4,64,2048]{3,2,1,0:T(8,128)(2,1)} %train_grads.1, bf16[1,2,64,3584]{3,2,1,0:T(8,128)(2,1)} %query_acts.1, bf16[1,2,64,2048]{3,2,1,0:T(8,128)(2,1)} %query_grads.1), custom_call_target="tpu_custom_call" | custom-call | tf_op jit(solution)/shard_map/pallas_call | solution.py:347
  48.7 1.2 %copy.9 = f32[2,8]{1,0:T(2,128)} copy(f32[2,8]{1,0:T(2,128)} %shard_map.73) | data formatting | bytes 128

commit v5 on v4

--- a/solution.py
+++ b/solution.py
@@ -13,10 +13,12 @@
 RIDGE_SCALE = 0.1
 LANES = 128
 TILE = 8
+RING = 4
 PLANES = 4
 FIRST_PLANE = 7
 SPOTS = 8
 PIVOTS = 16
+LATE = 6
 SLICE_ROWS = 4
 
 
@@ -71,7 +73,7 @@
     return jnp.concatenate([outer[: R1 // 2], outer[R1 // 2 :]], axis=1)
 
 
-def solve(gram, rhs):
+def solve(gram, late_rhs):
     total = gram.shape[0]
     high = PIVOTS // TILE
     sublane = lax.broadcasted_iota(jnp.int32, (TILE, LANES), 0)
@@ -83,8 +85,21 @@
     def down(tile, row):
         return jnp.broadcast_to(tile[row : row + 1, :], (TILE, LANES))
 
-    tiles = [gram[TILE * b : TILE * (b + 1)] for b in range(total // TILE)] + [rhs]
+    def eliminate(tile, start, rows):
+        inside = (lane >= start) & (lane < start + PIVOTS)
+        terms = [spread(tile, start + t) * down(rows[t // TILE], t % TILE) for t in range(PIVOTS)]
+        while len(terms) > 1:
+            terms = [a + b for a, b in zip(terms[::2], terms[1::2])]
+        return jnp.where(inside, 0.0, tile) - terms[0]
+
+    tiles = [gram[TILE * b : TILE * (b + 1)] for b in range(total // TILE)]
+    steps = []
+    rhs = None
     for start in range(0, total, PIVOTS):
+        if len(steps) == LATE:
+            rhs = late_rhs()
+            for step in steps:
+                rhs = eliminate(rhs, *step)
         first = start // TILE
         inside = (lane >= start) & (lane < start + PIVOTS)
         block = tiles[first : first + high]
@@ -104,13 +119,12 @@
                 column = [columns[c][i] - columns[t][i] * scaled for i in range(high)]
                 column[g] = jnp.where(here, scaled, column[g])
                 columns[c] = column
-        pivots = [down(rows[t // TILE], t % TILE) for t in range(PIVOTS)]
+        steps.append((start, rows))
         for i in range(first + high, len(tiles)):
-            terms = [spread(tiles[i], start + t) * pivots[t] for t in range(PIVOTS)]
-            while len(terms) > 1:
-                terms = [a + b for a, b in zip(terms[::2], terms[1::2])]
-            tiles[i] = jnp.where(inside, 0.0, tiles[i]) - terms[0]
-    return tiles[-1]
+            tiles[i] = eliminate(tiles[i], start, rows)
+        if rhs is not None:
+            rhs = eliminate(rhs, start, rows)
+    return rhs
 
 
 def kernel(
@@ -123,7 +137,14 @@
     members, ckpts = lax.axis_size("dp"), lax.axis_size("mp")
     trains, queries = train_acts.shape[1], query_acts.shape[1]
     spot = lax.rem(dp, SPOTS)
-    home = dp < SPOTS
+    plane_here, layer_here = dp // SPOTS, mp // RING
+    y = lax.rem(mp, RING)
+    layers = ckpts // RING
+    height = plane_here * layers + layer_here
+    home = (height >= 1) & (height <= layers)
+    mine = (layer_here + layers - 1) % layers * RING + y
+    to_plane, to_layer = (layer_here + 1) // layers, (layer_here + 1) % layers
+    in_first = plane_here == 0
 
     small = [
         pltpu.make_async_copy(salts, salts_here, load_sems.at[4]),
@@ -141,11 +162,8 @@
 
     barrier = pltpu.get_barrier_semaphore()
 
-    def greet_dp(peer):
-        pl.semaphore_signal(barrier, inc=1, device_id={"dp": peer}, device_id_type=MESH)
-
-    def greet_mp(peer):
-        pl.semaphore_signal(barrier, inc=1, device_id={"mp": peer}, device_id_type=MESH)
+    def greet(peer):
+        pl.semaphore_signal(barrier, inc=1, device_id=peer, device_id_type=MESH)
 
     def send(phase, source, target, device, arrival=None):
         copy = pltpu.make_async_remote_copy(
@@ -162,19 +180,27 @@
 
     @pl.when(home)
     def _():
-        @pl.loop(1, members)
-        def _(k):
-            greet_dp(lax.rem(dp + k, members))
-
-        @pl.loop(1, ckpts)
-        def _(k):
-            greet_mp(lax.rem(mp + k, ckpts))
-
-    @pl.when(jnp.logical_not(home))
-    def _():
-        @pl.loop(0, SPOTS)
-        def _(k):
-            greet_dp(k)
+        @pl.loop(0, members)
+        def _(k):
+            greet({"dp": k, "mp": mine})
+
+        @pl.loop(1, SPOTS)
+        def _(k):
+            greet({"dp": plane_here * SPOTS + lax.rem(spot + k, SPOTS), "mp": mp})
+
+    @pl.when(in_first)
+    def _():
+        @pl.loop(0, ckpts)
+        def _(k):
+            layer = k // RING + 1
+
+            @pl.when(jnp.logical_not(home) | (k != mine))
+            def _():
+                greet({"dp": layer // layers * SPOTS + spot, "mp": layer % layers * RING + k % RING})
+
+    @pl.when(jnp.logical_not(in_first))
+    def _():
+        greet({"dp": spot, "mp": mp})
 
     small[0].wait()
     sign_table(salts_here[0, 1], grads.shape[2], table_out)
@@ -201,51 +227,32 @@
         for j in range(SLICE_ROWS):
             train_send[:, j // 2, (j % 2) * trains + e, :] = rows[:, j]
 
-    plane_here = dp // SPOTS
-
-    def send_trains(first):
-        @pl.loop(first, SPOTS)
-        def _(k):
-            to = lax.rem(spot + k, SPOTS)
-            send(0, train_send.at[to], train_recv.at[dp], {"dp": to}, arrival=FIRST_PLANE + plane_here)
-
-    def send_queries(first):
-        @pl.loop(first, SPOTS)
-        def _(k):
-            to = lax.rem(spot + k, SPOTS)
-            send(1, query_send.at[to], query_recv.at[dp], {"dp": to})
-
-    def query_features():
-        loads[2].wait()
-        for e, rows in example_features(trains, queries):
-            for j in range(SLICE_ROWS):
-                query_send[:, j * queries + e, :] = rows[:, j]
-
-    @pl.when(jnp.logical_not(home))
-    def _():
-        pl.semaphore_wait(barrier, SPOTS)
-        send_trains(0)
-        query_features()
-        sent(0, train_send)
-        send_queries(0)
-        received(6, result_recv)
-        out_ref[...] = result_recv[0:queries, 0 : out_ref.shape[1]]
-        sent(1, query_send)
+    homes_wait = SPOTS - 1 + ckpts - in_first.astype(jnp.int32)
+    pl.semaphore_wait(barrier, SPOTS + jnp.where(home, homes_wait, 0) + jnp.where(in_first, PLANES - 1, 0))
+
+    @pl.loop(0, SPOTS)
+    def _(k):
+        to = lax.rem(spot + k, SPOTS)
+        there = {"dp": to_plane * SPOTS + to, "mp": to_layer * RING + y}
+        send(0, train_send.at[to], train_recv.at[dp], there, arrival=FIRST_PLANE + plane_here)
+
+    loads[2].wait()
+    for e, rows in example_features(trains, queries):
+        for j in range(SLICE_ROWS):
+            query_send[:, j * queries + e, :] = rows[:, j]
+    sent(0, train_send)
+
+    @pl.loop(0, SPOTS)
+    def _(k):
+        to = lax.rem(spot + k, SPOTS)
+        send(1, query_send.at[to], query_recv.at[dp], {"dp": to_plane * SPOTS + to, "mp": to_layer * RING + y})
 
     @pl.when(home)
     def _():
-        query_features()
-        pl.semaphore_wait(barrier, members - 1 + ckpts - 1)
-        send_trains(1)
-        send_queries(1)
-        train_recv[dp] = train_send[spot]
-        query_recv[dp] = query_send[spot]
-
         low = lax.broadcasted_iota(jnp.int32, (SPOTS // 2, TILE, LANES), 1) < trains
-        height = SPOTS * trains
+        high = SPOTS * trains
         for plane in (0, 1, 3, 2):
-            arrived = SPOTS if plane else SPOTS - 1
-            received(FIRST_PLANE + plane, train_recv.at[pl.ds(0, arrived)])
+            received(FIRST_PLANE + plane, train_recv.at[pl.ds(0, SPOTS)])
             for j in range(SLICE_ROWS):
                 pairs = train_recv[plane * SPOTS : (plane + 1) * SPOTS, j // 2]
                 pairs = pairs.reshape(SPOTS // 2, 2, TILE, LANES)
@@ -254,32 +261,35 @@
                     rows = jnp.where(low, even, pltpu.roll(odd, trains, 1))
                 else:
                     rows = jnp.where(low, pltpu.roll(even, trains, 1), odd)
-                high_part, low_part = halves(rows.reshape(height, LANES))
-                train_high[plane * height : (plane + 1) * height, j * LANES : (j + 1) * LANES] = high_part
-                train_low[plane * height : (plane + 1) * height, j * LANES : (j + 1) * LANES] = low_part
+                high_part, low_part = halves(rows.reshape(high, LANES))
+                train_high[plane * high : (plane + 1) * high, j * LANES : (j + 1) * LANES] = high_part
+                train_low[plane * high : (plane + 1) * high, j * LANES : (j + 1) * LANES] = low_part
         train_halves = train_high[...], train_low[...]
         gram_part[...] = product(train_halves, train_halves, 1)
         share = members * trains // SPOTS
 
+        def beside(to):
+            return {"dp": plane_here * SPOTS + to, "mp": mp}
+
         @pl.loop(1, SPOTS)
         def _(k):
             to = lax.rem(spot + k, SPOTS)
-            send(2, gram_part.at[pl.ds(pl.multiple_of(to * share, share), share)], gram_recv.at[spot], {"dp": to})
+            send(2, gram_part.at[pl.ds(pl.multiple_of(to * share, share), share)], gram_recv.at[spot], beside(to))
 
         gram_recv[spot] = gram_part[pl.ds(pl.multiple_of(spot * share, share), share), :]
 
         rest = pl.ds(0, SPOTS - 1)
         received(2, gram_recv.at[rest])
         gram_row[...] = jnp.sum(gram_recv[...], axis=0)
-        mine = pl.ds(pl.multiple_of(spot * share, share), share)
+        my_rows = pl.ds(pl.multiple_of(spot * share, share), share)
 
         @pl.loop(1, SPOTS)
         def _(k):
-            send(4, gram_row, gram_full.at[mine], {"dp": lax.rem(spot + k, SPOTS)})
-
-        gram_full[mine, :] = gram_row[...]
-
-        received(1, query_recv.at[pl.ds(0, members - 1)])
+            send(4, gram_row, gram_full.at[my_rows], beside(lax.rem(spot + k, SPOTS)))
+
+        gram_full[my_rows, :] = gram_row[...]
+
+        received(1, query_recv)
         planes = query_recv[...].reshape(PLANES, SPOTS, TILE, LANES)
         position = lax.broadcasted_iota(jnp.int32, (SPOTS, TILE, LANES), 1) // queries
         slices = []
@@ -296,45 +306,70 @@
         @pl.loop(1, SPOTS)
         def _(k):
             to = lax.rem(spot + k, SPOTS)
-            send(3, cross_part.at[to], cross_recv.at[spot], {"dp": to})
+            send(3, cross_part.at[to], cross_recv.at[spot], beside(to))
 
         cross_recv[spot] = cross_part[spot]
 
-        received(3, cross_recv.at[rest])
-        cross_terms = jnp.sum(cross_recv[...], axis=0)
         received(4, gram_full.at[pl.ds(0, share * (SPOTS - 1))])
+
+        def cross_terms():
+            received(3, cross_recv.at[rest])
+            return jnp.sum(cross_recv[...], axis=0)
 
         gram = gram_full[...]
         total = gram.shape[0]
         diagonal = lax.broadcasted_iota(jnp.int32, gram.shape, 0) == lax.broadcasted_iota(jnp.int32, gram.shape, 1)
         trace = jnp.sum(jnp.where(diagonal, gram, 0.0), axis=(0, 1), keepdims=True)
         ridge = RIDGE_SCALE * trace / total
-        system = jnp.where(diagonal, gram + ridge, gram)
-        solved = solve(system, cross_terms)
-
-        score_send[...] = solved
-
-        @pl.loop(1, ckpts)
-        def _(k):
-            send(5, score_send, score_recv.at[mp], {"mp": lax.rem(mp + k, ckpts)})
-
-        score_recv[mp] = solved
-        received(5, score_recv.at[pl.ds(0, ckpts - 1)])
-        summed = jnp.sum(score_recv[...], axis=0) * (total / ckpts)
-        width = out_ref.shape[1]
+        score_send[...] = solve(jnp.where(diagonal, gram + ridge, gram), cross_terms)
+
+        @pl.loop(0, ckpts)
+        def _(k):
+            @pl.when(jnp.logical_not(in_first) | (k != mp))
+            def _():
+                send(5, score_send, score_recv.at[mine], {"dp": spot, "mp": k})
+
+        @pl.when(in_first)
+        def _():
+            score_recv[mine] = score_send[...]
+            sent(5, score_recv.at[pl.ds(0, ckpts - 1)])
+
+        @pl.when(jnp.logical_not(in_first))
+        def _():
+            sent(5, score_recv)
+
+        sent(2, gram_recv.at[rest])
+        sent(3, cross_recv.at[rest])
+        sent(4, gram_full.at[pl.ds(0, share * (SPOTS - 1))])
+
+    width = out_ref.shape[1]
+
+    @pl.when(in_first)
+    def _():
+        @pl.when(home)
+        def _():
+            received(5, score_recv.at[pl.ds(0, ckpts - 1)])
+
+        @pl.when(jnp.logical_not(home))
+        def _():
+            received(5, score_recv)
+
+        scale = members * trains / ckpts
+        summed = jnp.sum(score_recv[...], axis=0) * scale
         summed = pltpu.roll(summed, lax.rem((ckpts - mp) * width, LANES), 1)
         for plane in range(1, PLANES):
             result_send[plane, 0:queries, :] = summed[plane * queries : (plane + 1) * queries]
             result_send[plane, queries:, :] = jnp.zeros((TILE - queries, LANES), jnp.float32)
-            send(6, result_send.at[plane], result_recv, {"dp": plane * SPOTS + spot})
+            send(6, result_send.at[plane], result_recv, {"dp": plane * SPOTS + spot, "mp": mp})
         out_ref[...] = summed[0:queries, 0:width]
-        sent(0, train_send.at[rest])
-        sent(1, query_send.at[rest])
-        sent(2, gram_recv.at[rest])
-        sent(3, cross_recv.at[rest])
-        sent(4, gram_full.at[pl.ds(0, share * (SPOTS - 1))])
-        sent(5, score_recv.at[pl.ds(0, ckpts - 1)])
         sent(6, result_send.at[pl.ds(0, PLANES - 1)])
+
+    @pl.when(jnp.logical_not(in_first))
+    def _():
+        received(6, result_recv)
+        out_ref[...] = result_recv[0:queries, 0:width]
+
+    sent(1, query_send)
 
 
 def shards(train_acts, train_grads, query_acts, query_grads, train_lengths, query_lengths, proj_salts):

time: 50.1 us -> 47.5 us (0.948)
  Pallas kernels: 48.7 us -> 46.1 us
    pallas_call x1, Pallas kernels: 48.7 us -> 46.1 us  [shards(): pl.pallas_call(kernel, out_shape=jax.ShapeDtypeStruct((queries, total //...]
where the time goes in v5:
time: 47.5 us; the launch traced here: 47.3 us
  Pallas kernels  46.1 us (97%)
  local copies, waits for them, and re-layouts  1.24 us (3%)
    pallas_call x1, Pallas kernels, shards(): pl.pallas_call(kernel, out_shape=jax.ShapeDtypeStruct((queries, total //...  46.1 us
    unnamed x1, local copies, waits for them, and re-layouts  1.24 us

profile of v5, /device:TPU:1, one launch (start us, length us, event | category | flops | bytes accessed | tf_op | source)
XLA Modules:
  0.0 47.3 jit_solution(11921493327277278420)
XLA Ops:
  0.0 46.1 %shard_map.73 = f32[2,8]{1,0:T(2,128)} custom-call(s32[1,2]{1,0:T(1,128)} %salts.1, s32[4]{0:T(128)} %train_lengths.1, s32[2]{0:T(128)} %query_lengths.1, bf16[1,4,64,3584]{3,2,1,0:T(8,128)(2,1)} %train_acts.1, bf16[1,4,64,2048]{3,2,1,0:T(8,128)(2,1)} %train_grads.1, bf16[1,2,64,3584]{3,2,1,0:T(8,128)(2,1)} %query_acts.1, bf16[1,2,64,2048]{3,2,1,0:T(8,128)(2,1)} %query_grads.1), custom_call_target="tpu_custom_call" | custom-call | tf_op jit(solution)/shard_map/pallas_call | solution.py:382
  46.1 1.2 %copy.9 = f32[2,8]{1,0:T(2,128)} copy(f32[2,8]{1,0:T(2,128)} %shard_map.73) | data formatting | bytes 128

commit v6 on v5

--- a/solution.py
+++ b/solution.py
@@ -140,11 +140,9 @@
     plane_here, layer_here = dp // SPOTS, mp // RING
     y = lax.rem(mp, RING)
     layers = ckpts // RING
-    height = plane_here * layers + layer_here
-    home = (height >= 1) & (height <= layers)
+    home = plane_here == 0
     mine = (layer_here + layers - 1) % layers * RING + y
-    to_plane, to_layer = (layer_here + 1) // layers, (layer_here + 1) % layers
-    in_first = plane_here == 0
+    home_of_mine = (layer_here + 1) % layers * RING + y
 
     small = [
         pltpu.make_async_copy(salts, salts_here, load_sems.at[4]),
@@ -186,19 +184,13 @@
 
         @pl.loop(1, SPOTS)
         def _(k):
-            greet({"dp": plane_here * SPOTS + lax.rem(spot + k, SPOTS), "mp": mp})
-
-    @pl.when(in_first)
-    def _():
-        @pl.loop(0, ckpts)
-        def _(k):
-            layer = k // RING + 1
-
-            @pl.when(jnp.logical_not(home) | (k != mine))
-            def _():
-                greet({"dp": layer // layers * SPOTS + spot, "mp": layer % layers * RING + k % RING})
-
-    @pl.when(jnp.logical_not(in_first))
+            greet({"dp": lax.rem(spot + k, SPOTS), "mp": mp})
+
+        @pl.loop(1, ckpts)
+        def _(k):
+            greet({"dp": dp, "mp": lax.rem(mp + k, ckpts)})
+
+    @pl.when(jnp.logical_not(home))
     def _():
         greet({"dp": spot, "mp": mp})
 
@@ -206,7 +198,7 @@
     sign_table(salts_here[0, 1], grads.shape[2], table_out)
     sign_table(salts_here[0, 0], acts.shape[2], table_in)
 
-    length = acts.shape[1]
+    length, width = acts.shape[1], out_ref.shape[1]
 
     def example_features(first, count):
         some = pl.ds(first, count)
@@ -227,13 +219,12 @@
         for j in range(SLICE_ROWS):
             train_send[:, j // 2, (j % 2) * trains + e, :] = rows[:, j]
 
-    homes_wait = SPOTS - 1 + ckpts - in_first.astype(jnp.int32)
-    pl.semaphore_wait(barrier, SPOTS + jnp.where(home, homes_wait, 0) + jnp.where(in_first, PLANES - 1, 0))
+    pl.semaphore_wait(barrier, SPOTS + jnp.where(home, SPOTS - 1 + ckpts - 1 + PLANES - 1, 0))
 
     @pl.loop(0, SPOTS)
     def _(k):
         to = lax.rem(spot + k, SPOTS)
-        there = {"dp": to_plane * SPOTS + to, "mp": to_layer * RING + y}
+        there = {"dp": to, "mp": home_of_mine}
         send(0, train_send.at[to], train_recv.at[dp], there, arrival=FIRST_PLANE + plane_here)
 
     loads[2].wait()
@@ -245,7 +236,7 @@
     @pl.loop(0, SPOTS)
     def _(k):
         to = lax.rem(spot + k, SPOTS)
-        send(1, query_send.at[to], query_recv.at[dp], {"dp": to_plane * SPOTS + to, "mp": to_layer * RING + y})
+        send(1, query_send.at[to], query_recv.at[dp], {"dp": to, "mp": home_of_mine})
 
     @pl.when(home)
     def _():
@@ -269,7 +260,7 @@
         share = members * trains // SPOTS
 
         def beside(to):
-            return {"dp": plane_here * SPOTS + to, "mp": mp}
+            return {"dp": to, "mp": mp}
 
         @pl.loop(1, SPOTS)
         def _(k):
@@ -323,37 +314,12 @@
         ridge = RIDGE_SCALE * trace / total
         score_send[...] = solve(jnp.where(diagonal, gram + ridge, gram), cross_terms)
 
-        @pl.loop(0, ckpts)
-        def _(k):
-            @pl.when(jnp.logical_not(in_first) | (k != mp))
-            def _():
-                send(5, score_send, score_recv.at[mine], {"dp": spot, "mp": k})
-
-        @pl.when(in_first)
-        def _():
-            score_recv[mine] = score_send[...]
-            sent(5, score_recv.at[pl.ds(0, ckpts - 1)])
-
-        @pl.when(jnp.logical_not(in_first))
-        def _():
-            sent(5, score_recv)
-
-        sent(2, gram_recv.at[rest])
-        sent(3, cross_recv.at[rest])
-        sent(4, gram_full.at[pl.ds(0, share * (SPOTS - 1))])
-
-    width = out_ref.shape[1]
-
-    @pl.when(in_first)
-    def _():
-        @pl.when(home)
-        def _():
-            received(5, score_recv.at[pl.ds(0, ckpts - 1)])
-
-        @pl.when(jnp.logical_not(home))
-        def _():
-            received(5, score_recv)
-
+        @pl.loop(1, ckpts)
+        def _(k):
+            send(5, score_send, score_recv.at[mine], {"dp": dp, "mp": lax.rem(mp + k, ckpts)})
+
+        score_recv[mine] = score_send[...]
+        received(5, score_recv.at[pl.ds(0, ckpts - 1)])
         scale = members * trains / ckpts
         summed = jnp.sum(score_recv[...], axis=0) * scale
         summed = pltpu.roll(summed, lax.rem((ckpts - mp) * width, LANES), 1)
@@ -362,9 +328,13 @@
             result_send[plane, queries:, :] = jnp.zeros((TILE - queries, LANES), jnp.float32)
             send(6, result_send.at[plane], result_recv, {"dp": plane * SPOTS + spot, "mp": mp})
         out_ref[...] = summed[0:queries, 0:width]
+        sent(2, gram_recv.at[rest])
+        sent(3, cross_recv.at[rest])
+        sent(4, gram_full.at[pl.ds(0, share * (SPOTS - 1))])
+        sent(5, score_recv.at[pl.ds(0, ckpts - 1)])
         sent(6, result_send.at[pl.ds(0, PLANES - 1)])
 
-    @pl.when(jnp.logical_not(in_first))
+    @pl.when(jnp.logical_not(home))
     def _():
         received(6, result_recv)
         out_ref[...] = result_recv[0:queries, 0:width]

time: 47.5 us -> 46.4 us (0.977)
  Pallas kernels: 46.1 us -> 45 us
    pallas_call x1, Pallas kernels: 46.1 us -> 45 us  [shards(): pl.pallas_call(kernel, out_shape=jax.ShapeDtypeStruct((queries, total //...]
where the time goes in v6:
time: 46.4 us; the launch traced here: 46.2 us
  Pallas kernels  45 us (97%)
  local copies, waits for them, and re-layouts  1.24 us (3%)
    pallas_call x1, Pallas kernels, shards(): pl.pallas_call(kernel, out_shape=jax.ShapeDtypeStruct((queries, total //...  45 us
    unnamed x1, local copies, waits for them, and re-layouts  1.24 us

profile of v6, /device:TPU:1, one launch (start us, length us, event | category | flops | bytes accessed | tf_op | source)
XLA Modules:
  0.0 46.2 jit_solution(1653838075884524075)
XLA Ops:
  0.0 45.0 %shard_map.73 = f32[2,8]{1,0:T(2,128)} custom-call(s32[1,2]{1,0:T(1,128)} %salts.1, s32[4]{0:T(128)} %train_lengths.1, s32[2]{0:T(128)} %query_lengths.1, bf16[1,4,64,3584]{3,2,1,0:T(8,128)(2,1)} %train_acts.1, bf16[1,4,64,2048]{3,2,1,0:T(8,128)(2,1)} %train_grads.1, bf16[1,2,64,3584]{3,2,1,0:T(8,128)(2,1)} %query_acts.1, bf16[1,2,64,2048]{3,2,1,0:T(8,128)(2,1)} %query_grads.1), custom_call_target="tpu_custom_call" | custom-call | tf_op jit(solution)/shard_map/pallas_call | solution.py:352
  45.0 1.2 %copy.9 = f32[2,8]{1,0:T(2,128)} copy(f32[2,8]{1,0:T(2,128)} %shard_map.73) | data formatting | bytes 128

commit v7 on v6

--- a/solution.py
+++ b/solution.py
@@ -15,10 +15,10 @@
 TILE = 8
 RING = 4
 PLANES = 4
-FIRST_PLANE = 7
+QUERY_ROW = 7
 SPOTS = 8
+CORES = 2
 PIVOTS = 16
-LATE = 6
 SLICE_ROWS = 4
 
 
@@ -73,8 +73,8 @@
     return jnp.concatenate([outer[: R1 // 2], outer[R1 // 2 :]], axis=1)
 
 
-def solve(gram, late_rhs):
-    total = gram.shape[0]
+def invert(system_ref):
+    total = system_ref.shape[0]
     high = PIVOTS // TILE
     sublane = lax.broadcasted_iota(jnp.int32, (TILE, LANES), 0)
     lane = lax.broadcasted_iota(jnp.int32, (TILE, LANES), 1)
@@ -85,21 +85,8 @@
     def down(tile, row):
         return jnp.broadcast_to(tile[row : row + 1, :], (TILE, LANES))
 
-    def eliminate(tile, start, rows):
-        inside = (lane >= start) & (lane < start + PIVOTS)
-        terms = [spread(tile, start + t) * down(rows[t // TILE], t % TILE) for t in range(PIVOTS)]
-        while len(terms) > 1:
-            terms = [a + b for a, b in zip(terms[::2], terms[1::2])]
-        return jnp.where(inside, 0.0, tile) - terms[0]
-
-    tiles = [gram[TILE * b : TILE * (b + 1)] for b in range(total // TILE)]
-    steps = []
-    rhs = None
+    tiles = [system_ref[TILE * b : TILE * (b + 1), :] for b in range(total // TILE)]
     for start in range(0, total, PIVOTS):
-        if len(steps) == LATE:
-            rhs = late_rhs()
-            for step in steps:
-                rhs = eliminate(rhs, *step)
         first = start // TILE
         inside = (lane >= start) & (lane < start + PIVOTS)
         block = tiles[first : first + high]
@@ -110,28 +97,32 @@
         for t in range(PIVOTS):
             g, r = t // TILE, t % TILE
             here = sublane == r
-            inverse = 1.0 / down(columns[t][g], r)
-            pivot_row = down(rows[g], r) * inverse
+            scale = 1.0 / down(columns[t][g], r)
+            pivot_row = down(rows[g], r) * scale
             rows = [rows[i] - columns[t][i] * pivot_row for i in range(high)]
             rows[g] = jnp.where(here, pivot_row, rows[g])
             for c in range(t + 1, PIVOTS):
-                scaled = down(columns[c][g], r) * inverse
+                scaled = down(columns[c][g], r) * scale
                 column = [columns[c][i] - columns[t][i] * scaled for i in range(high)]
                 column[g] = jnp.where(here, scaled, column[g])
                 columns[c] = column
-        steps.append((start, rows))
-        for i in range(first + high, len(tiles)):
-            tiles[i] = eliminate(tiles[i], start, rows)
-        if rhs is not None:
-            rhs = eliminate(rhs, start, rows)
-    return rhs
+        pivots = [down(rows[t // TILE], t % TILE) for t in range(PIVOTS)]
+        for i in [*range(first + high, len(tiles)), *range(first)]:
+            terms = [spread(tiles[i], start + t) * pivots[t] for t in range(PIVOTS)]
+            while len(terms) > 1:
+                terms = [a + b for a, b in zip(terms[::2], terms[1::2])]
+            tiles[i] = jnp.where(inside, 0.0, tiles[i]) - terms[0]
+        for g in range(high):
+            tiles[first + g] = -rows[g]
+    for b, tile in enumerate(tiles):
+        system_ref[TILE * b : TILE * (b + 1), :] = tile
 
 
 def kernel(
     salts, train_lengths, query_lengths, train_acts, train_grads, query_acts, query_grads, out_ref,
-    acts, grads, table_in, table_out, train_send, query_send, train_recv, query_recv, train_high, train_low,
+    acts, grads, table_in, table_out, train_send, query_send, query_row, train_recv, query_recv, train_high, train_low,
     gram_part, cross_part, gram_recv, cross_recv, gram_row, gram_full, score_send, score_recv, result_send, result_recv,
-    salts_here, train_lengths_here, query_lengths_here, load_sems, send_sems, recv_sems,
+    salts_here, train_lengths_here, query_lengths_here, load_sems, send_sems, recv_sems, here_sem, go_sem,
 ):
     dp, mp = lax.axis_index("dp"), lax.axis_index("mp")
     members, ckpts = lax.axis_size("dp"), lax.axis_size("mp")
@@ -142,6 +133,25 @@
     layers = ckpts // RING
     home = plane_here == 0
     mine = (layer_here + layers - 1) % layers * RING + y
+    last = layers - 1
+    late = plane_here == PLANES - 2
+    tail_up = (plane_here == PLANES - 1) & (layer_here == last)
+    yields_up = (plane_here == PLANES - 1) & (layer_here < last) | late & (layer_here == last)
+    tail_down = late & (layer_here == 0)
+    yields_down = late & (layer_here > 0) & (layer_here < last)
+    tail, yields = tail_up, yields_up
+    awaited = jnp.where(tail_up, layers, 0)
+    tail_of_mine = {
+        "dp": (PLANES - 2 + yields_up.astype(jnp.int32)) * SPOTS + spot,
+        "mp": jnp.where(yields_up, last, 0) * RING + y,
+    }
+
+    def before(k):
+        up = {"plane": PLANES - 1 - k // last, "layer": k}
+        down = {"plane": PLANES - 2, "layer": k + 1}
+        plane, layer = (jnp.where(tail_up, up[name], down[name]) for name in ("plane", "layer"))
+        return {"dp": plane * SPOTS + spot, "mp": layer * RING + y}
+
     home_of_mine = (layer_here + 1) % layers * RING + y
 
     small = [
@@ -182,10 +192,6 @@
         def _(k):
             greet({"dp": k, "mp": mine})
 
-        @pl.loop(1, SPOTS)
-        def _(k):
-            greet({"dp": lax.rem(spot + k, SPOTS), "mp": mp})
-
         @pl.loop(1, ckpts)
         def _(k):
             greet({"dp": dp, "mp": lax.rem(mp + k, ckpts)})
@@ -193,6 +199,16 @@
     @pl.when(jnp.logical_not(home))
     def _():
         greet({"dp": spot, "mp": mp})
+
+    @pl.loop(1, SPOTS)
+    def _(k):
+        greet({"dp": plane_here * SPOTS + lax.rem(spot + k, SPOTS), "mp": mp})
+
+    @pl.when(tail)
+    def _():
+        @pl.loop(0, awaited)
+        def _(k):
+            greet(before(k))
 
     small[0].wait()
     sign_table(salts_here[0, 1], grads.shape[2], table_out)
@@ -219,31 +235,55 @@
         for j in range(SLICE_ROWS):
             train_send[:, j // 2, (j % 2) * trains + e, :] = rows[:, j]
 
-    pl.semaphore_wait(barrier, SPOTS + jnp.where(home, SPOTS - 1 + ckpts - 1 + PLANES - 1, 0))
+    pl.semaphore_wait(barrier, 2 * SPOTS - 1 + jnp.where(home, ckpts - 1 + PLANES - 1, 0) + yields.astype(jnp.int32))
+
+    @pl.when(yields)
+    def _():
+        pl.semaphore_signal(here_sem, inc=1, device_id=tail_of_mine, device_id_type=MESH)
+
+
+    def to_others(action):
+        x, core, chips = spot // CORES, lax.rem(spot, CORES), SPOTS // CORES
+        for away, other in ((2, 0), (2, 1), (1, 0), (1, 1), (3, 0), (3, 1), (0, 1)):
+            to = lax.rem(x + away, chips) * CORES + lax.rem(core + other, CORES)
+            action(to, {"dp": plane_here * SPOTS + to, "mp": mp})
 
     @pl.loop(0, SPOTS)
     def _(k):
         to = lax.rem(spot + k, SPOTS)
         there = {"dp": to, "mp": home_of_mine}
-        send(0, train_send.at[to], train_recv.at[dp], there, arrival=FIRST_PLANE + plane_here)
+        send(0, train_send.at[to], train_recv.at[dp], there, arrival=QUERY_ROW + 1 + plane_here)
 
     loads[2].wait()
     for e, rows in example_features(trains, queries):
         for j in range(SLICE_ROWS):
             query_send[:, j * queries + e, :] = rows[:, j]
+    to_others(lambda to, device: send(QUERY_ROW, query_send.at[to], query_row.at[spot], device))
+    query_row[spot] = query_send[spot]
+    received(QUERY_ROW, query_row.at[pl.ds(0, SPOTS - 1)])
     sent(0, train_send)
 
-    @pl.loop(0, SPOTS)
-    def _(k):
-        to = lax.rem(spot + k, SPOTS)
-        send(1, query_send.at[to], query_recv.at[dp], {"dp": to, "mp": home_of_mine})
+    @pl.when(tail)
+    def _():
+        pl.semaphore_wait(here_sem, awaited)
+
+        @pl.loop(0, awaited)
+        def _(k):
+            pl.semaphore_signal(go_sem, inc=1, device_id=before(k), device_id_type=MESH)
+
+    @pl.when(yields)
+    def _():
+        pl.semaphore_wait(go_sem, 1)
+
+    in_plane = pl.ds(pl.multiple_of(plane_here * SPOTS, SPOTS), SPOTS)
+    send(1, query_row, query_recv.at[in_plane], {"dp": spot, "mp": home_of_mine})
 
     @pl.when(home)
     def _():
         low = lax.broadcasted_iota(jnp.int32, (SPOTS // 2, TILE, LANES), 1) < trains
         high = SPOTS * trains
         for plane in (0, 1, 3, 2):
-            received(FIRST_PLANE + plane, train_recv.at[pl.ds(0, SPOTS)])
+            received(QUERY_ROW + 1 + plane, train_recv.at[pl.ds(0, SPOTS)])
             for j in range(SLICE_ROWS):
                 pairs = train_recv[plane * SPOTS : (plane + 1) * SPOTS, j // 2]
                 pairs = pairs.reshape(SPOTS // 2, 2, TILE, LANES)
@@ -259,13 +299,10 @@
         gram_part[...] = product(train_halves, train_halves, 1)
         share = members * trains // SPOTS
 
-        def beside(to):
-            return {"dp": to, "mp": mp}
-
-        @pl.loop(1, SPOTS)
-        def _(k):
-            to = lax.rem(spot + k, SPOTS)
-            send(2, gram_part.at[pl.ds(pl.multiple_of(to * share, share), share)], gram_recv.at[spot], beside(to))
+        def send_part(to, device):
+            send(2, gram_part.at[pl.ds(pl.multiple_of(to * share, share), share)], gram_recv.at[spot], device)
+
+        to_others(send_part)
 
         gram_recv[spot] = gram_part[pl.ds(pl.multiple_of(spot * share, share), share), :]
 
@@ -274,10 +311,7 @@
         gram_row[...] = jnp.sum(gram_recv[...], axis=0)
         my_rows = pl.ds(pl.multiple_of(spot * share, share), share)
 
-        @pl.loop(1, SPOTS)
-        def _(k):
-            send(4, gram_row, gram_full.at[my_rows], beside(lax.rem(spot + k, SPOTS)))
-
+        to_others(lambda to, device: send(4, gram_row, gram_full.at[my_rows], device))
         gram_full[my_rows, :] = gram_row[...]
 
         received(1, query_recv)
@@ -294,30 +328,27 @@
         cross = product(halves(jnp.concatenate(slices, axis=1)), (train_high[...], train_low[...]), 1)
         cross_part[...] = cross.reshape(SPOTS, TILE, LANES)
 
-        @pl.loop(1, SPOTS)
-        def _(k):
-            to = lax.rem(spot + k, SPOTS)
-            send(3, cross_part.at[to], cross_recv.at[spot], beside(to))
-
+        to_others(lambda to, device: send(3, cross_part.at[to], cross_recv.at[spot], device))
         cross_recv[spot] = cross_part[spot]
 
         received(4, gram_full.at[pl.ds(0, share * (SPOTS - 1))])
-
-        def cross_terms():
-            received(3, cross_recv.at[rest])
-            return jnp.sum(cross_recv[...], axis=0)
 
         gram = gram_full[...]
         total = gram.shape[0]
         diagonal = lax.broadcasted_iota(jnp.int32, gram.shape, 0) == lax.broadcasted_iota(jnp.int32, gram.shape, 1)
         trace = jnp.sum(jnp.where(diagonal, gram, 0.0), axis=(0, 1), keepdims=True)
         ridge = RIDGE_SCALE * trace / total
-        score_send[...] = solve(jnp.where(diagonal, gram + ridge, gram), cross_terms)
-
-        @pl.loop(1, ckpts)
-        def _(k):
-            send(5, score_send, score_recv.at[mine], {"dp": dp, "mp": lax.rem(mp + k, ckpts)})
-
+        gram_full[...] = jnp.where(diagonal, gram + ridge, gram)
+        invert(gram_full)
+        received(3, cross_recv.at[rest])
+        cross_terms = halves(jnp.sum(cross_recv[...], axis=0))
+        score_send[...] = product(cross_terms, halves(gram_full[...]), 1)
+
+        for around in (2, 1, 3, 0):
+            for up in (2, 3, 1, 0):
+                if around or up:
+                    to = lax.rem(layer_here + up, layers) * RING + lax.rem(y + around, RING)
+                    send(5, score_send, score_recv.at[mine], {"dp": dp, "mp": to})
         score_recv[mine] = score_send[...]
         received(5, score_recv.at[pl.ds(0, ckpts - 1)])
         scale = members * trains / ckpts
@@ -339,7 +370,8 @@
         received(6, result_recv)
         out_ref[...] = result_recv[0:queries, 0:width]
 
-    sent(1, query_send)
+    sent(1, query_row)
+    sent(QUERY_ROW, query_send.at[pl.ds(0, SPOTS - 1)])
 
 
 def shards(train_acts, train_grads, query_acts, query_grads, train_lengths, query_lengths, proj_salts):
@@ -361,6 +393,7 @@
             pltpu.VMEM((out_width // 2, LANES), bf16),
             pltpu.VMEM((SPOTS, SLICE_ROWS // 2, TILE, LANES), f32),
             pltpu.VMEM((SPOTS, TILE, LANES), f32),
+            pltpu.VMEM((SPOTS, TILE, LANES), f32),
             pltpu.VMEM((members, SLICE_ROWS // 2, TILE, LANES), f32),
             pltpu.VMEM((members, TILE, LANES), f32),
             pltpu.VMEM((total, SLICE_ROWS * LANES), bf16),
@@ -379,8 +412,10 @@
             pltpu.SMEM((trains,), i32),
             pltpu.SMEM((queries,), i32),
             pltpu.SemaphoreType.DMA((7,)),
-            pltpu.SemaphoreType.DMA((FIRST_PLANE,)),
-            pltpu.SemaphoreType.DMA((FIRST_PLANE + PLANES,)),
+            pltpu.SemaphoreType.DMA((QUERY_ROW + 1,)),
+            pltpu.SemaphoreType.DMA((QUERY_ROW + 1 + PLANES,)),
+            pltpu.SemaphoreType.REGULAR,
+            pltpu.SemaphoreType.REGULAR,
         ],
         compiler_params=pltpu.CompilerParams(
             collective_id=0, has_side_effects=True, vmem_limit_bytes=64 * 1024 * 1024

time: 46.4 us -> 44.9 us (0.968)
  Pallas kernels: 45 us -> 43.6 us
    pallas_call x1, Pallas kernels: 45 us -> 43.6 us  [shards(): pl.pallas_call(kernel, out_shape=jax.ShapeDtypeStruct((queries, total //...]
where the time goes in v7:
time: 44.9 us; the launch traced here: 44.8 us
  Pallas kernels  43.6 us (97%)
  local copies, waits for them, and re-layouts  1.24 us (3%)
    pallas_call x1, Pallas kernels, shards(): pl.pallas_call(kernel, out_shape=jax.ShapeDtypeStruct((queries, total //...  43.6 us
    unnamed x1, local copies, waits for them, and re-layouts  1.24 us

profile of v7, /device:TPU:1, one launch (start us, length us, event | category | flops | bytes accessed | tf_op | source)
XLA Modules:
  0.0 44.8 jit_solution(8564239377792733646)
XLA Ops:
  0.0 43.6 %shard_map.73 = f32[2,8]{1,0:T(2,128)} custom-call(s32[1,2]{1,0:T(1,128)} %salts.1, s32[4]{0:T(128)} %train_lengths.1, s32[2]{0:T(128)} %query_lengths.1, bf16[1,4,64,3584]{3,2,1,0:T(8,128)(2,1)} %train_acts.1, bf16[1,4,64,2048]{3,2,1,0:T(8,128)(2,1)} %train_grads.1, bf16[1,2,64,3584]{3,2,1,0:T(8,128)(2,1)} %query_acts.1, bf16[1,2,64,2048]{3,2,1,0:T(8,128)(2,1)} %query_grads.1), custom_call_target="tpu_custom_call" | custom-call | tf_op jit(solution)/shard_map/pallas_call | solution.py:384
  43.6 1.2 %copy.9 = f32[2,8]{1,0:T(2,128)} copy(f32[2,8]{1,0:T(2,128)} %shard_map.73) | data formatting | bytes 128

commit v8 on v7

--- a/solution.py
+++ b/solution.py
@@ -18,6 +18,7 @@
 QUERY_ROW = 7
 SPOTS = 8
 CORES = 2
+LATE = 6
 PIVOTS = 16
 SLICE_ROWS = 4
 
@@ -73,7 +74,7 @@
     return jnp.concatenate([outer[: R1 // 2], outer[R1 // 2 :]], axis=1)
 
 
-def invert(system_ref):
+def solve(system_ref, steps_ref, late_rhs):
     total = system_ref.shape[0]
     high = PIVOTS // TILE
     sublane = lax.broadcasted_iota(jnp.int32, (TILE, LANES), 0)
@@ -85,9 +86,27 @@
     def down(tile, row):
         return jnp.broadcast_to(tile[row : row + 1, :], (TILE, LANES))
 
-    tiles = [system_ref[TILE * b : TILE * (b + 1), :] for b in range(total // TILE)]
+    def eliminate(tile, start, rows):
+        inside = (lane >= start) & (lane < start + PIVOTS)
+        terms = [spread(tile, start + t) * down(rows[t // TILE], t % TILE) for t in range(PIVOTS)]
+        while len(terms) > 1:
+            terms = [a + b for a, b in zip(terms[::2], terms[1::2])]
+        return jnp.where(inside, 0.0, tile) - terms[0]
+
+    def rows_at(ref, first, count):
+        return [ref[TILE * b : TILE * (b + 1), :] for b in range(first, first + count)]
+
+    tiles = rows_at(system_ref, 0, total // TILE)
+    rhs = None
     for start in range(0, total, PIVOTS):
         first = start // TILE
+        if start == LATE * PIVOTS:
+            for b in range(first, len(tiles)):
+                system_ref[TILE * b : TILE * (b + 1), :] = tiles[b]
+            rhs = late_rhs()
+            tiles[first:] = rows_at(system_ref, first, len(tiles) - first)
+            for done in range(0, start, PIVOTS):
+                rhs = eliminate(rhs, done, rows_at(steps_ref, done // TILE, high))
         inside = (lane >= start) & (lane < start + PIVOTS)
         block = tiles[first : first + high]
         columns = [[spread(tile, start + t) for tile in block] for t in range(PIVOTS)]
@@ -106,23 +125,21 @@
                 column = [columns[c][i] - columns[t][i] * scaled for i in range(high)]
                 column[g] = jnp.where(here, scaled, column[g])
                 columns[c] = column
-        pivots = [down(rows[t // TILE], t % TILE) for t in range(PIVOTS)]
-        for i in [*range(first + high, len(tiles)), *range(first)]:
-            terms = [spread(tiles[i], start + t) * pivots[t] for t in range(PIVOTS)]
-            while len(terms) > 1:
-                terms = [a + b for a, b in zip(terms[::2], terms[1::2])]
-            tiles[i] = jnp.where(inside, 0.0, tiles[i]) - terms[0]
-        for g in range(high):
-            tiles[first + g] = -rows[g]
-    for b, tile in enumerate(tiles):
-        system_ref[TILE * b : TILE * (b + 1), :] = tile
+        for i in range(first + high, len(tiles)):
+            tiles[i] = eliminate(tiles[i], start, rows)
+        if rhs is not None:
+            rhs = eliminate(rhs, start, rows)
+        elif start < LATE * PIVOTS:
+            for g in range(high):
+                steps_ref[TILE * (first + g) : TILE * (first + g + 1), :] = rows[g]
+    return rhs
 
 
 def kernel(
     salts, train_lengths, query_lengths, train_acts, train_grads, query_acts, query_grads, out_ref,
     acts, grads, table_in, table_out, train_send, query_send, query_row, train_recv, query_recv, train_high, train_low,
-    gram_part, cross_part, gram_recv, cross_recv, gram_row, gram_full, score_send, score_recv, result_send, result_recv,
-    salts_here, train_lengths_here, query_lengths_here, load_sems, send_sems, recv_sems, here_sem, go_sem,
+    gram_part, cross_part, gram_recv, cross_recv, gram_row, gram_full, steps, score_send, score_recv, result_send, result_recv,
+    salts_here, train_lengths_here, query_lengths_here, load_sems, send_sems, recv_sems, here_sem, go_sem, reach_sem,
 ):
     dp, mp = lax.axis_index("dp"), lax.axis_index("mp")
     members, ckpts = lax.axis_size("dp"), lax.axis_size("mp")
@@ -139,8 +156,8 @@
     yields_up = (plane_here == PLANES - 1) & (layer_here < last) | late & (layer_here == last)
     tail_down = late & (layer_here == 0)
     yields_down = late & (layer_here > 0) & (layer_here < last)
-    tail, yields = tail_up, yields_up
-    awaited = jnp.where(tail_up, layers, 0)
+    tail, yields = tail_up | tail_down, yields_up | yields_down
+    awaited = jnp.where(tail_up, layers, jnp.where(tail_down, layers - 2, 0))
     tail_of_mine = {
         "dp": (PLANES - 2 + yields_up.astype(jnp.int32)) * SPOTS + spot,
         "mp": jnp.where(yields_up, last, 0) * RING + y,
@@ -196,9 +213,8 @@
         def _(k):
             greet({"dp": dp, "mp": lax.rem(mp + k, ckpts)})
 
-    @pl.when(jnp.logical_not(home))
-    def _():
-        greet({"dp": spot, "mp": mp})
+        for plane in range(1, PLANES):
+            greet({"dp": plane * SPOTS + spot, "mp": mp})
 
     @pl.loop(1, SPOTS)
     def _(k):
@@ -235,7 +251,11 @@
         for j in range(SLICE_ROWS):
             train_send[:, j // 2, (j % 2) * trains + e, :] = rows[:, j]
 
-    pl.semaphore_wait(barrier, 2 * SPOTS - 1 + jnp.where(home, ckpts - 1 + PLANES - 1, 0) + yields.astype(jnp.int32))
+    pl.semaphore_wait(barrier, 2 * SPOTS - 1 + jnp.where(home, ckpts - 1, 1) + yields.astype(jnp.int32))
+
+    @pl.when(jnp.logical_not(home))
+    def _():
+        pl.semaphore_signal(reach_sem, inc=1, device_id={"dp": spot, "mp": mp}, device_id_type=MESH)
 
     @pl.when(yields)
     def _():
@@ -339,10 +359,12 @@
         trace = jnp.sum(jnp.where(diagonal, gram, 0.0), axis=(0, 1), keepdims=True)
         ridge = RIDGE_SCALE * trace / total
         gram_full[...] = jnp.where(diagonal, gram + ridge, gram)
-        invert(gram_full)
-        received(3, cross_recv.at[rest])
-        cross_terms = halves(jnp.sum(cross_recv[...], axis=0))
-        score_send[...] = product(cross_terms, halves(gram_full[...]), 1)
+
+        def cross_terms():
+            received(3, cross_recv.at[rest])
+            return jnp.sum(cross_recv[...], axis=0)
+
+        score_send[...] = solve(gram_full, steps, cross_terms)
 
         for around in (2, 1, 3, 0):
             for up in (2, 3, 1, 0):
@@ -354,6 +376,7 @@
         scale = members * trains / ckpts
         summed = jnp.sum(score_recv[...], axis=0) * scale
         summed = pltpu.roll(summed, lax.rem((ckpts - mp) * width, LANES), 1)
+        pl.semaphore_wait(reach_sem, PLANES - 1)
         for plane in range(1, PLANES):
             result_send[plane, 0:queries, :] = summed[plane * queries : (plane + 1) * queries]
             result_send[plane, queries:, :] = jnp.zeros((TILE - queries, LANES), jnp.float32)
@@ -404,6 +427,7 @@
             pltpu.VMEM((SPOTS, TILE, LANES), f32),
             pltpu.VMEM((total // SPOTS, LANES), f32),
             pltpu.VMEM((total, LANES), f32),
+            pltpu.VMEM((total, LANES), f32),
             pltpu.VMEM((TILE, LANES), f32),
             pltpu.VMEM((ckpts, TILE, LANES), f32),
             pltpu.VMEM((PLANES, TILE, LANES), f32),
@@ -416,6 +440,7 @@
             pltpu.SemaphoreType.DMA((QUERY_ROW + 1 + PLANES,)),
             pltpu.SemaphoreType.REGULAR,
             pltpu.SemaphoreType.REGULAR,
+            pltpu.SemaphoreType.REGULAR,
         ],
         compiler_params=pltpu.CompilerParams(
             collective_id=0, has_side_effects=True, vmem_limit_bytes=64 * 1024 * 1024

time: 44.9 us -> 44.2 us (0.984)
  Pallas kernels: 43.6 us -> 42.8 us
    pallas_call x1, Pallas kernels: 43.6 us -> 42.8 us  [shards(): pl.pallas_call(kernel, out_shape=jax.ShapeDtypeStruct((queries, total //...]
where the time goes in v8:
time: 44.2 us; the launch traced here: 44 us
  Pallas kernels  42.8 us (97%)
  local copies, waits for them, and re-layouts  1.24 us (3%)
    pallas_call x1, Pallas kernels, shards(): pl.pallas_call(kernel, out_shape=jax.ShapeDtypeStruct((queries, total //...  42.8 us
    unnamed x1, local copies, waits for them, and re-layouts  1.24 us

profile of v8, /device:TPU:1, one launch (start us, length us, event | category | flops | bytes accessed | tf_op | source)
XLA Modules:
  0.0 44.0 jit_solution(8469962728490089161)
XLA Ops:
  0.0 42.8 %shard_map.73 = f32[2,8]{1,0:T(2,128)} custom-call(s32[1,2]{1,0:T(1,128)} %salts.1, s32[4]{0:T(128)} %train_lengths.1, s32[2]{0:T(128)} %query_lengths.1, bf16[1,4,64,3584]{3,2,1,0:T(8,128)(2,1)} %train_acts.1, bf16[1,4,64,2048]{3,2,1,0:T(8,128)(2,1)} %train_grads.1, bf16[1,2,64,3584]{3,2,1,0:T(8,128)(2,1)} %query_acts.1, bf16[1,2,64,2048]{3,2,1,0:T(8,128)(2,1)} %query_grads.1), custom_call_target="tpu_custom_call" | custom-call | tf_op jit(solution)/shard_map/pallas_call | solution.py:407
  42.8 1.2 %copy.9 = f32[2,8]{1,0:T(2,128)} copy(f32[2,8]{1,0:T(2,128)} %shard_map.73) | data formatting | bytes 128

commit v9 on v8

--- a/solution.py
+++ b/solution.py
@@ -139,7 +139,7 @@
     salts, train_lengths, query_lengths, train_acts, train_grads, query_acts, query_grads, out_ref,
     acts, grads, table_in, table_out, train_send, query_send, query_row, train_recv, query_recv, train_high, train_low,
     gram_part, cross_part, gram_recv, cross_recv, gram_row, gram_full, steps, score_send, score_recv, result_send, result_recv,
-    salts_here, train_lengths_here, query_lengths_here, load_sems, send_sems, recv_sems, here_sem, go_sem, reach_sem,
+    out_here, projections, salts_here, train_lengths_here, query_lengths_here, load_sems, send_sems, recv_sems, here_sem, go_sem, reach_sem,
 ):
     dp, mp = lax.axis_index("dp"), lax.axis_index("mp")
     members, ckpts = lax.axis_size("dp"), lax.axis_size("mp")
@@ -171,6 +171,8 @@
 
     home_of_mine = (layer_here + 1) % layers * RING + y
 
+    half = acts.shape[2] // 2
+    first_half, second_half = pl.ds(0, half), pl.ds(half, half)
     small = [
         pltpu.make_async_copy(salts, salts_here, load_sems.at[4]),
         pltpu.make_async_copy(train_lengths, train_lengths_here, load_sems.at[5]),
@@ -178,11 +180,12 @@
     ]
     loads = [
         pltpu.make_async_copy(train_grads.at[0], grads.at[pl.ds(0, trains)], load_sems.at[0]),
-        pltpu.make_async_copy(train_acts.at[0], acts.at[pl.ds(0, trains)], load_sems.at[1]),
+        pltpu.make_async_copy(train_acts.at[0, :, :, first_half], acts.at[pl.ds(0, trains), :, first_half], load_sems.at[1]),
         pltpu.make_async_copy(query_grads.at[0], grads.at[pl.ds(trains, queries)], load_sems.at[2]),
         pltpu.make_async_copy(query_acts.at[0], acts.at[pl.ds(trains, queries)], load_sems.at[3]),
+        pltpu.make_async_copy(train_acts.at[0, :, :, second_half], acts.at[pl.ds(0, trains), :, second_half], load_sems.at[7]),
     ]
-    for load in small + loads[:2]:
+    for load in [*small, *loads[:2], loads[4]]:
         load.start()
 
     barrier = pltpu.get_barrier_semaphore()
@@ -231,12 +234,24 @@
     sign_table(salts_here[0, 0], acts.shape[2], table_in)
 
     length, width = acts.shape[1], out_ref.shape[1]
+    write = pltpu.make_async_copy(out_here, out_ref, load_sems.at[8])
 
     def example_features(first, count):
         some = pl.ds(first, count)
         right = projected(grads[some].reshape(count * length, grads.shape[2]), table_out[...])
-        loads[1 if first == 0 else 3].wait()
-        left = projected(acts[some].reshape(count * length, acts.shape[2]), table_in[...])
+        if first == 0:
+            projections[0, :, 0:R2] = right
+            loads[1].wait()
+            tokens = acts[some, :, first_half].reshape(count * length, half)
+            projections[1] = jnp.dot(tokens, table_in[...], preferred_element_type=jnp.float32)
+            loads[4].wait()
+            tokens = acts[some, :, second_half].reshape(count * length, half)
+            left = jnp.dot(tokens, table_in[...], preferred_element_type=jnp.float32)
+            left = projections[1, :, 0:R1] + left[:, R1:]
+            right = projections[0, :, 0:R2]
+        else:
+            loads[3].wait()
+            left = projected(acts[some].reshape(count * length, acts.shape[2]), table_in[...])
         for e in range(count):
             tokens = slice(e * length, (e + 1) * length)
             used = train_lengths_here[e] if first == 0 else query_lengths_here[e]
@@ -376,12 +391,13 @@
         scale = members * trains / ckpts
         summed = jnp.sum(score_recv[...], axis=0) * scale
         summed = pltpu.roll(summed, lax.rem((ckpts - mp) * width, LANES), 1)
+        out_here[...] = summed[0:queries, 0:width]
+        write.start()
         pl.semaphore_wait(reach_sem, PLANES - 1)
         for plane in range(1, PLANES):
             result_send[plane, 0:queries, :] = summed[plane * queries : (plane + 1) * queries]
             result_send[plane, queries:, :] = jnp.zeros((TILE - queries, LANES), jnp.float32)
             send(6, result_send.at[plane], result_recv, {"dp": plane * SPOTS + spot, "mp": mp})
-        out_ref[...] = summed[0:queries, 0:width]
         sent(2, gram_recv.at[rest])
         sent(3, cross_recv.at[rest])
         sent(4, gram_full.at[pl.ds(0, share * (SPOTS - 1))])
@@ -391,8 +407,10 @@
     @pl.when(jnp.logical_not(home))
     def _():
         received(6, result_recv)
-        out_ref[...] = result_recv[0:queries, 0:width]
-
+        out_here[...] = result_recv[0:queries, 0:width]
+        write.start()
+
+    write.wait()
     sent(1, query_row)
     sent(QUERY_ROW, query_send.at[pl.ds(0, SPOTS - 1)])
 
@@ -408,7 +426,7 @@
         kernel,
         out_shape=jax.ShapeDtypeStruct((queries, total // ckpts), f32),
         in_specs=[pl.BlockSpec(memory_space=pltpu.HBM)] * 7,
-        out_specs=pl.BlockSpec(memory_space=pltpu.VMEM),
+        out_specs=pl.BlockSpec(memory_space=pltpu.HBM),
         scratch_shapes=[
             pltpu.VMEM((trains + queries, length, width), bf16),
             pltpu.VMEM((trains + queries, length, out_width), bf16),
@@ -432,10 +450,12 @@
             pltpu.VMEM((ckpts, TILE, LANES), f32),
             pltpu.VMEM((PLANES, TILE, LANES), f32),
             pltpu.VMEM((TILE, LANES), f32),
+            pltpu.VMEM((queries, total // ckpts), f32),
+            pltpu.VMEM((2, trains * length, LANES), f32),
             pltpu.SMEM((1, 2), i32),
             pltpu.SMEM((trains,), i32),
             pltpu.SMEM((queries,), i32),
-            pltpu.SemaphoreType.DMA((7,)),
+            pltpu.SemaphoreType.DMA((9,)),
             pltpu.SemaphoreType.DMA((QUERY_ROW + 1,)),
             pltpu.SemaphoreType.DMA((QUERY_ROW + 1 + PLANES,)),
             pltpu.SemaphoreType.REGULAR,

time: 44.2 us -> 43.8 us (level)
  no operation moved by 1% of the time
where the time goes in v9:
time: 43.8 us; the launch traced here: 43.7 us
  Pallas kernels  42.4 us (97%)
  local copies, waits for them, and re-layouts  1.24 us (3%)
    pallas_call x1, Pallas kernels, shards(): pl.pallas_call(kernel, out_shape=jax.ShapeDtypeStruct((queries, total //...  42.4 us
    unnamed x1, local copies, waits for them, and re-layouts  1.24 us

profile of v9, /device:TPU:1, one launch (start us, length us, event | category | flops | bytes accessed | tf_op | source)
XLA Modules:
  0.0 43.7 jit_solution(5376244367291626238)
XLA Ops:
  0.0 42.4 %shard_map.73 = f32[2,8]{1,0:T(2,128)} custom-call(s32[1,2]{1,0:T(1,128)} %salts.1, s32[4]{0:T(128)} %train_lengths.1, s32[2]{0:T(128)} %query_lengths.1, bf16[1,4,64,3584]{3,2,1,0:T(8,128)(2,1)} %train_acts.1, bf16[1,4,64,2048]{3,2,1,0:T(8,128)(2,1)} %train_grads.1, bf16[1,2,64,3584]{3,2,1,0:T(8,128)(2,1)} %query_acts.1, bf16[1,2,64,2048]{3,2,1,0:T(8,128)(2,1)} %query_grads.1), custom_call_target="tpu_custom_call" | custom-call | tf_op jit(solution)/shard_map/pallas_call | solution.py:425
  42.4 1.2 %copy.9 = f32[2,8]{1,0:T(2,128)} copy(f32[2,8]{1,0:T(2,128)} %shard_map.73) | data formatting | bytes 128

commit v10 on v9

--- a/solution.py
+++ b/solution.py
@@ -317,7 +317,11 @@
     def _():
         low = lax.broadcasted_iota(jnp.int32, (SPOTS // 2, TILE, LANES), 1) < trains
         high = SPOTS * trains
-        for plane in (0, 1, 3, 2):
+        for plane in range(PLANES):
+            if plane == PLANES - 1:
+                known = plane * high
+                earlier = train_high[0:known, :], train_low[0:known, :]
+                gram_part[0:known, 0:known] = product(earlier, earlier, 1)
             received(QUERY_ROW + 1 + plane, train_recv.at[pl.ds(0, SPOTS)])
             for j in range(SLICE_ROWS):
                 pairs = train_recv[plane * SPOTS : (plane + 1) * SPOTS, j // 2]
@@ -331,7 +335,9 @@
                 train_high[plane * high : (plane + 1) * high, j * LANES : (j + 1) * LANES] = high_part
                 train_low[plane * high : (plane + 1) * high, j * LANES : (j + 1) * LANES] = low_part
         train_halves = train_high[...], train_low[...]
-        gram_part[...] = product(train_halves, train_halves, 1)
+        latest = train_high[known:, :], train_low[known:, :]
+        gram_part[known:, :] = product(latest, train_halves, 1)
+        gram_part[0:known, known:] = product((train_high[0:known, :], train_low[0:known, :]), latest, 1)
         share = members * trains // SPOTS
 
         def send_part(to, device):

time: 43.8 us -> 43.8 us (level)
  no operation moved by 1% of the time
where the time goes in v10:
time: 43.8 us; the launch traced here: 43.7 us
  Pallas kernels  42.5 us (97%)
  local copies, waits for them, and re-layouts  1.24 us (3%)
    pallas_call x1, Pallas kernels, shards(): pl.pallas_call(kernel, out_shape=jax.ShapeDtypeStruct((queries, total //...  42.5 us
    unnamed x1, local copies, waits for them, and re-layouts  1.24 us

profile of v10, /device:TPU:1, one launch (start us, length us, event | category | flops | bytes accessed | tf_op | source)
XLA Modules:
  0.0 43.7 jit_solution(17320294531245703840)
XLA Ops:
  0.0 42.5 %shard_map.73 = f32[2,8]{1,0:T(2,128)} custom-call(s32[1,2]{1,0:T(1,128)} %salts.1, s32[4]{0:T(128)} %train_lengths.1, s32[2]{0:T(128)} %query_lengths.1, bf16[1,4,64,3584]{3,2,1,0:T(8,128)(2,1)} %train_acts.1, bf16[1,4,64,2048]{3,2,1,0:T(8,128)(2,1)} %train_grads.1, bf16[1,2,64,3584]{3,2,1,0:T(8,128)(2,1)} %query_acts.1, bf16[1,2,64,2048]{3,2,1,0:T(8,128)(2,1)} %query_grads.1), custom_call_target="tpu_custom_call" | custom-call | tf_op jit(solution)/shard_map/pallas_call | solution.py:431
  42.5 1.2 %copy.9 = f32[2,8]{1,0:T(2,128)} copy(f32[2,8]{1,0:T(2,128)} %shard_map.73) | data formatting | bytes 128
